TPU v7x, 512 devices: a whole 4x8x8 slice. The times are simulated.
512 devices in a mesh: ctx: 64 (over z, y_lo, core), tp: 8 (over y_hi, x).
Axes of the slice: x: 4, y: 8 (y_hi: 2, y_lo: 4; y = y_hi * 4 + y_lo), z: 8, core: 2. Of those that a mesh axis runs over, the one named last changes fastest.
Arguments:
- queries: bfloat16 [512, 65536], P('tp', 'ctx'), may hold values from -6 to 6
- keys: bfloat16 [512, 65536], P('tp', 'ctx'), may hold values from -6 to 6
- values: bfloat16 [512, 65536], P('tp', 'ctx'), may hold values from -6 to 6
- grad_out: bfloat16 [512, 65536], P('tp', 'ctx'), may hold values from -6 to 6
- residues: float32 [512, 16], P('tp'), may hold values from -1.5 to 1.5
- decay_rate: float32 [512, 16], P('tp'), may hold values from 7.6293946e-07 to 0.033
- skip_gain: float32 [512], P('tp'), may hold values from -4 to 4
Outputs:
- grad_queries: bfloat16 [512, 65536], P('tp', 'ctx')
- grad_keys: bfloat16 [512, 65536], P('tp', 'ctx')
- grad_values: bfloat16 [512, 65536], P('tp', 'ctx')
- grad_residues: float32 [512, 16], P('tp')
- grad_skip: float32 [512], P('tp')
All inputs are finite; a program needn't handle non-finite values.
Results may differ from a plain program's by a relative error of at most 0.0035.
Values may be sent and summed in bfloat16 or wider, within the bound.
No kernel may reach another device: no remote copies, remote signals or barrier semaphores. Data moves between devices by JAX's collectives and lax.ppermute only.
A program may use at most 64 MiB of HBM per device.

v0:
```python
import math

import jax
import jax.numpy as jnp
from jax import lax
from jax.sharding import PartitionSpec as P

BLOCK = 128


HIGH = lax.Precision.HIGHEST


def shortened(x):

    def short(part):
        return part.astype(jnp.bfloat16) if part.dtype == jnp.float32 else part

    return jax.tree.map(short, x)


def powers(rate, offsets):
    return jnp.exp(-rate[:, :, None] * offsets[None, None, :])


def masked_decay(rate, scale, count, shift):
    position = jnp.arange(count)
    differ = position[:, None] - position[None, :] - shift
    keeper = differ >= 0
    safe = jnp.where(keeper, differ, 0).astype(jnp.float32)
    return jnp.where(
        keeper[None, None], jnp.exp(-rate[:, :, None, None] * (scale * safe)[None, None]), 0.0
    )


def summaries(inputs, rate):
    width = inputs.shape[3]
    blocks = inputs.shape[2]
    offsets = (width - 1 - jnp.arange(width)).astype(jnp.float32)
    block_sum = jnp.einsum("csnj,cmj->csnm", inputs, powers(rate, offsets), precision=HIGH)
    within = masked_decay(rate, width, blocks, 0)
    return jnp.einsum("cmnk,cskm->csnm", within, block_sum, precision=HIGH)


def finish(inputs, ends, start_state, rate, weight, skip):
    chans, segs, blocks, width = inputs.shape
    seg_len = blocks * width
    outer = masked_decay(rate, seg_len, segs, 1)
    seg_in = jnp.einsum("cmsr,crm->csm", outer, ends[:, :, -1, :], precision=HIGH)
    seg_decay = jnp.transpose(
        powers(rate, seg_len * jnp.arange(segs).astype(jnp.float32)), (0, 2, 1)
    )
    seg_in = seg_in + seg_decay * start_state[:, None, :]
    block_decay = jnp.transpose(
        powers(rate, width * jnp.arange(blocks).astype(jnp.float32)), (0, 2, 1)
    )
    earlier = jnp.concatenate([jnp.zeros_like(ends[:, :, :1, :]), ends[:, :, :-1, :]], axis=2)
    previous = earlier + block_decay[:, None, :, :] * seg_in[:, :, None, :]
    lead = weight[:, :, None] * powers(rate, jnp.arange(1, width + 1).astype(jnp.float32))
    output = jnp.einsum("csnm,cmi->csni", previous, lead, precision=HIGH)
    taps = jnp.einsum(
        "cm,cmd->cd", weight, powers(rate, jnp.arange(width).astype(jnp.float32)), precision=HIGH
    )
    position = jnp.arange(width)
    differ = position[:, None] - position[None, :]
    lower = differ >= 0
    toeplitz = jnp.where(lower[None], taps[:, jnp.where(lower, differ, 0)], 0.0)
    output = output + jnp.einsum("cij,csnj->csni", toeplitz, inputs, precision=HIGH)
    output = output + skip[:, None, None, None] * inputs
    return (output, previous)


def mode_sums(inputs, previous, signal, rate):
    width = inputs.shape[3]
    position = jnp.arange(width)
    differ = position[:, None] - position[None, :]
    lower = differ >= 0
    safe = jnp.where(lower, differ, 0).astype(jnp.float32)
    leading = jnp.arange(1, width + 1).astype(jnp.float32)

    def one_mode(pieces):
        rate_col, prev_col = pieces
        decay = jnp.where(lower[None], jnp.exp(-rate_col[:, None, None] * safe[None]), 0.0)
        inner = jnp.einsum("cij,csnj->csni", decay, inputs, precision=HIGH)
        inner = (
            inner
            + jnp.exp(-rate_col[:, None] * leading[None])[:, None, None, :] * prev_col[..., None]
        )
        return jnp.sum(signal * inner, axis=(1, 2, 3))

    sums = lax.map(one_mode, (rate.T, jnp.moveaxis(previous, 3, 0)))
    return sums.T


def local_backward(
    queries, keys, values, grad_out, rate, weight, skip, enter_forward, enter_adjoint
):
    units = keys.astype(jnp.float32) * values.astype(jnp.float32)
    signal = grad_out.astype(jnp.float32) * queries.astype(jnp.float32)
    ends = summaries(units, rate)
    start_state = enter_forward(ends[:, -1, -1, :])
    mixed, previous = finish(units, ends, start_state, rate, weight, skip)
    flipped = jnp.flip(signal, axis=(1, 2, 3))
    back_ends = summaries(flipped, rate)
    back_start = enter_adjoint(back_ends[:, -1, -1, :])
    back_flip, unused = finish(flipped, back_ends, back_start, rate, weight, skip)
    back = jnp.flip(back_flip, axis=(1, 2, 3))
    grad_queries = (grad_out.astype(jnp.float32) * mixed).astype(jnp.bfloat16)
    grad_keys = (back * values.astype(jnp.float32)).astype(jnp.bfloat16)
    grad_values = (back * keys.astype(jnp.float32)).astype(jnp.bfloat16)
    totals = mode_sums(units, previous, signal, rate)
    direct = jnp.sum(signal * units, axis=(1, 2, 3))
    return (grad_queries, grad_keys, grad_values, totals, direct)


def shards(queries, keys, values, grad_out, residues, decay_rate, skip_gain):
    all_gain = jnp.sqrt(-jnp.expm1(-2.0 * decay_rate))
    all_weight = residues * all_gain
    chans, tok_local = queries.shape
    parts = lax.axis_size("ctx")
    total_tokens = tok_local * parts
    share = chans // parts
    offset = lax.axis_index("ctx") * share
    rate = lax.dynamic_slice_in_dim(decay_rate, offset, share, 0)
    weight = lax.dynamic_slice_in_dim(all_weight, offset, share, 0)
    skip = lax.dynamic_slice_in_dim(skip_gain, offset, share, 0)
    gathered = (
        lax.all_to_all(queries, "ctx", split_axis=0, concat_axis=1, tiled=True),
        lax.all_to_all(keys, "ctx", split_axis=0, concat_axis=1, tiled=True),
        lax.all_to_all(values, "ctx", split_axis=0, concat_axis=1, tiled=True),
        lax.all_to_all(grad_out, "ctx", split_axis=0, concat_axis=1, tiled=True),
    )
    shaped = tuple((piece.reshape(share, parts, tok_local // BLOCK, BLOCK) for piece in gathered))

    def no_state(summary):
        return jnp.zeros_like(summary)

    grad_q, grad_k, grad_v, totals, direct = local_backward(
        shaped[0], shaped[1], shaped[2], shaped[3], rate, weight, skip, no_state, no_state
    )
    flat = tuple((piece.reshape(share, total_tokens) for piece in (grad_q, grad_k, grad_v)))
    grad_q, grad_k, grad_v = jax.tree.map(
        lambda part, own: part.astype(own.dtype),
        lax.all_to_all(shortened(flat), "ctx", split_axis=1, concat_axis=0, tiled=True),
        flat,
    )
    summed_modes, summed_skip = (
        lax.all_gather(totals, "ctx", axis=0, tiled=True),
        lax.all_gather(direct, "ctx", axis=0, tiled=True),
    )
    norm = math.sqrt(total_tokens)
    grad_residues = all_gain * summed_modes / norm
    grad_skip = summed_skip / norm
    return (grad_q, grad_k, grad_v, grad_residues, grad_skip)


def solution(mesh):
    in_specs = (
        P("tp", "ctx"),
        P("tp", "ctx"),
        P("tp", "ctx"),
        P("tp", "ctx"),
        P("tp", None),
        P("tp", None),
        P("tp"),
    )
    out_specs = (P("tp", "ctx"), P("tp", "ctx"), P("tp", "ctx"), P("tp", None), P("tp"))
    return jax.shard_map(shards, mesh=mesh, in_specs=in_specs, out_specs=out_specs, check_vma=False)
```

profile of v0, /device:TPU:6, one launch (start us, length us, event | category | flops | bytes accessed | tf_op | source)
XLA Modules:
  0.0 421.6 jit_solution(15893385652941160763)
XLA Ops:
  1.1 1.6 reduce.7
  3.5 14.5 %all-to-all-start = ((bf16[64,2,512]{2,1,0:T(2,128)(2,1)}), bf16[64,2,512]{2,1,0:T(2,128)(2,1)S(1)}, u32[]{:S(2)}, u32[]{:S(2)}) async-start(bf16[64,2,512]{2,1,0:T(2,128)(2,1)} %reshape.894), calls=%async_computation | async-start | bytes 262144 | tf_op jit(solution)/shard_map/all_to_all | solution.py:131
  20.6 8.2 %all-to-all-done = bf16[64,2,512]{2,1,0:T(2,128)(2,1)S(1)} async-done(((bf16[64,2,512]{2,1,0:T(2,128)(2,1)}), bf16[64,2,512]{2,1,0:T(2,128)(2,1)S(1)}, u32[]{:S(2)}, u32[]{:S(2)}) %all-to-all-start) | async-done | bytes 131104 | tf_op jit(solution)/shard_map/all_to_all | solution.py:131
  28.7 4.6 %all-to-all-start.2 = ((bf16[64,2,512]{2,1,0:T(2,128)(2,1)}), bf16[64,2,512]{2,1,0:T(2,128)(2,1)S(1)}, u32[]{:S(2)}, u32[]{:S(2)}) async-start(bf16[64,2,512]{2,1,0:T(2,128)(2,1)} %reshape.896), calls=%async_computation.2 | async-start | bytes 262144 | tf_op jit(solution)/shard_map/all_to_all | solution.py:130
  34.9 9.3 %all-to-all-done.2 = bf16[64,2,512]{2,1,0:T(2,128)(2,1)S(1)} async-done(((bf16[64,2,512]{2,1,0:T(2,128)(2,1)}), bf16[64,2,512]{2,1,0:T(2,128)(2,1)S(1)}, u32[]{:S(2)}, u32[]{:S(2)}) %all-to-all-start.2) | async-done | bytes 131104 | tf_op jit(solution)/shard_map/all_to_all | solution.py:130
  44.1 4.6 %all-to-all-start.1 = ((bf16[64,2,512]{2,1,0:T(2,128)(2,1)}), bf16[64,2,512]{2,1,0:T(2,128)(2,1)S(1)}, u32[]{:S(2)}, u32[]{:S(2)}) async-start(bf16[64,2,512]{2,1,0:T(2,128)(2,1)} %reshape.898), calls=%async_computation.1 | async-start | bytes 262144 | tf_op jit(solution)/shard_map/all_to_all | solution.py:129
  50.2 9.3 %all-to-all-done.1 = bf16[64,2,512]{2,1,0:T(2,128)(2,1)S(1)} async-done(((bf16[64,2,512]{2,1,0:T(2,128)(2,1)}), bf16[64,2,512]{2,1,0:T(2,128)(2,1)S(1)}, u32[]{:S(2)}, u32[]{:S(2)}) %all-to-all-start.1) | async-done | bytes 131104 | tf_op jit(solution)/shard_map/all_to_all | solution.py:129
  59.5 4.8 %all-to-all-start.4 = ((bf16[64,2,512]{2,1,0:T(2,128)(2,1)}), bf16[64,2,512]{2,1,0:T(2,128)(2,1)S(1)}, u32[]{:S(2)}, u32[]{:S(2)}) async-start(bf16[64,2,512]{2,1,0:T(2,128)(2,1)} %reshape.902), calls=%async_computation.4 | async-start | bytes 262144 | tf_op jit(solution)/shard_map/all_to_all | solution.py:128
  65.6 97.2 %gather_fusion = f32[16384]{0:T(1024)S(1)} fusion(f32[128]{0:T(128)S(1)} %convolution_bitcast_fusion.3, s32[16384]{0:T(1024)S(1)} %fusion.44), kind=kCustom, calls=%fused_computation | custom fusion | bytes 196608 | tf_op jit(solution)/shard_map/gather | solution.py:67
  173.5 58.7 %while.11 = (s32[]{:T(128)}, f32[16,1]{0,1:T(1,128)S(1)}, f32[1,64,8,128]{3,1,2,0:T(8,128)S(1)}, f32[16,1]{0,1:T(1,128)S(1)}, f32[1,64,8,128]{3,1,2,0:T(8,128)S(...) while((s32[]{:T(128)}, f32[16,1]{0,1:T(1,128)S(1)}, f32[1,64,8,128]{3,1,2,0:T(8,128)S(1)}, ...), condition=%wide.region_2.3_spmd.clone, body=%wide.region_0.2_spmd.clone.sunk | while | flops 101024128 | bytes 531581 | solution.py:91
  174.8 1.7 fusion.116
  178.4 1.7 fusion.116
  182.1 1.7 fusion.116
  185.7 1.7 fusion.116
  189.4 1.7 fusion.116
  193.1 1.7 fusion.116
  196.7 1.7 fusion.116
  200.4 1.7 fusion.116
  204.1 1.7 fusion.116
  207.8 1.7 fusion.116
  211.4 1.7 fusion.116
  215.1 1.7 fusion.116
  218.8 1.7 fusion.116
  222.4 1.7 fusion.116
  226.1 1.7 fusion.116
  229.8 1.7 fusion.116
  234.4 10.4 %all-to-all-start.6 = ((bf16[64,2,512]{2,1,0:T(2,128)(2,1)}), bf16[64,2,512]{2,1,0:T(2,128)(2,1)S(1)}, u32[]{:S(2)}, u32[]{:S(2)}) async-start(bf16[64,2,512]{2,1,0:T(2,128)(2,1)} %reshape.906), calls=%async_computation.6 | async-start | bytes 262144 | tf_op jit(solution)/shard_map/all_to_all | solution.py:144
  249.8 5.7 %all-to-all-done.6 = bf16[64,2,512]{2,1,0:T(2,128)(2,1)S(1)} async-done(((bf16[64,2,512]{2,1,0:T(2,128)(2,1)}), bf16[64,2,512]{2,1,0:T(2,128)(2,1)S(1)}, u32[]{:S(2)}, u32[]{:S(2)}) %all-to-all-start.6) | async-done | bytes 131104 | tf_op jit(solution)/shard_map/all_to_all | solution.py:144
  255.6 4.9 %all-to-all-start.5 = ((bf16[64,2,512]{2,1,0:T(2,128)(2,1)}), bf16[64,2,512]{2,1,0:T(2,128)(2,1)S(1)}, u32[]{:S(2)}, u32[]{:S(2)}) async-start(bf16[64,2,512]{2,1,0:T(2,128)(2,1)} %reshape.904), calls=%async_computation.5 | async-start | bytes 262144 | tf_op jit(solution)/shard_map/all_to_all | solution.py:144
  260.5 141.2 %all-reduce.4 = (f32[1024]{0:T(1024)S(1)}, f32[64]{0:T(128)S(1)}) all-reduce(f32[1024]{0:T(1024)S(1)} %bitcast_dynamic-update-slice_fusion, f32[64]{0:T(128)S(1)} %dynamic-update-slice.1), channel_id=2, replica_groups=mesh['ctx'=64,'tp'=8] {'ctx'}, use_global_device_ids=true, to_apply=%add.2 | all-reduce | flops 1088 | bytes 8704
  404.7 5.3 %all-to-all-start.3 = ((bf16[64,2,512]{2,1,0:T(2,128)(2,1)}), bf16[64,2,512]{2,1,0:T(2,128)(2,1)S(1)}, u32[]{:S(2)}, u32[]{:S(2)}) async-start(bf16[64,2,512]{2,1,0:T(2,128)(2,1)} %reshape.900), calls=%async_computation.3 | async-start | bytes 262144 | tf_op jit(solution)/shard_map/all_to_all | solution.py:144
  412.8 7.9 %all-to-all-done.3 = bf16[64,2,512]{2,1,0:T(2,128)(2,1)S(1)} async-done(((bf16[64,2,512]{2,1,0:T(2,128)(2,1)}), bf16[64,2,512]{2,1,0:T(2,128)(2,1)S(1)}, u32[]{:S(2)}, u32[]{:S(2)}) %all-to-all-start.3) | async-done | bytes 131104 | tf_op jit(solution)/shard_map/all_to_all | solution.py:144
  (160 shorter events, 63.2 us)
Async XLA Ops:
  3.5 14.6 %copy-start.3 = (f32[64,16]{0,1:T(8,128)S(1)}, f32[64,16]{0,1:T(8,128)}, u32[]{:S(2)}) copy-start(f32[64,16]{0,1:T(8,128)} %param.14) | copy-start | bytes 12292
  3.5 14.7 %copy-start.4 = (f32[64,16]{0,1:T(8,128)S(1)}, f32[64,16]{0,1:T(8,128)}, u32[]{:S(2)}) copy-start(f32[64,16]{0,1:T(8,128)} %param.13) | copy-start | bytes 12292
  3.5 25.3 %all-to-all-start = ((bf16[64,2,512]{2,1,0:T(2,128)(2,1)}), bf16[64,2,512]{2,1,0:T(2,128)(2,1)S(1)}, u32[]{:S(2)}, u32[]{:S(2)}) async-start(bf16[64,2,512]{2,1,0:T(2,128)(2,1)} %reshape.894), calls=%async_computation | async-start | bytes 262144 | tf_op jit(solution)/shard_map/all_to_all | solution.py:131
  18.0 0.9 copy-start
  20.6 12.8 %copy-start.1 = (bf16[64,1024]{1,0:T(8,128)(2,1)S(1)}, bf16[64,1024]{1,0:T(8,128)(2,1)}, u32[]{:S(2)}) copy-start(bf16[64,1024]{1,0:T(8,128)(2,1)} %param.10) | copy-start | bytes 393220
  28.7 15.4 %all-to-all-start.2 = ((bf16[64,2,512]{2,1,0:T(2,128)(2,1)}), bf16[64,2,512]{2,1,0:T(2,128)(2,1)S(1)}, u32[]{:S(2)}, u32[]{:S(2)}) async-start(bf16[64,2,512]{2,1,0:T(2,128)(2,1)} %reshape.896), calls=%async_computation.2 | async-start | bytes 262144 | tf_op jit(solution)/shard_map/all_to_all | solution.py:130
  34.9 13.9 %copy-start.2 = (bf16[64,1024]{1,0:T(8,128)(2,1)S(1)}, bf16[64,1024]{1,0:T(8,128)(2,1)}, u32[]{:S(2)}) copy-start(bf16[64,1024]{1,0:T(8,128)(2,1)} %param.9) | copy-start | bytes 393220
  44.1 15.4 %all-to-all-start.1 = ((bf16[64,2,512]{2,1,0:T(2,128)(2,1)}), bf16[64,2,512]{2,1,0:T(2,128)(2,1)S(1)}, u32[]{:S(2)}, u32[]{:S(2)}) async-start(bf16[64,2,512]{2,1,0:T(2,128)(2,1)} %reshape.898), calls=%async_computation.1 | async-start | bytes 262144 | tf_op jit(solution)/shard_map/all_to_all | solution.py:129
  59.5 106.2 %all-to-all-start.4 = ((bf16[64,2,512]{2,1,0:T(2,128)(2,1)}), bf16[64,2,512]{2,1,0:T(2,128)(2,1)S(1)}, u32[]{:S(2)}, u32[]{:S(2)}) async-start(bf16[64,2,512]{2,1,0:T(2,128)(2,1)} %reshape.902), calls=%async_computation.4 | async-start | bytes 262144 | tf_op jit(solution)/shard_map/all_to_all | solution.py:128
  64.4 0.7 copy-start.5
  234.4 21.2 %all-to-all-start.6 = ((bf16[64,2,512]{2,1,0:T(2,128)(2,1)}), bf16[64,2,512]{2,1,0:T(2,128)(2,1)S(1)}, u32[]{:S(2)}, u32[]{:S(2)}) async-start(bf16[64,2,512]{2,1,0:T(2,128)(2,1)} %reshape.906), calls=%async_computation.6 | async-start | bytes 262144 | tf_op jit(solution)/shard_map/all_to_all | solution.py:144
  255.6 149.1 %all-to-all-start.5 = ((bf16[64,2,512]{2,1,0:T(2,128)(2,1)}), bf16[64,2,512]{2,1,0:T(2,128)(2,1)S(1)}, u32[]{:S(2)}, u32[]{:S(2)}) async-start(bf16[64,2,512]{2,1,0:T(2,128)(2,1)} %reshape.904), calls=%async_computation.5 | async-start | bytes 262144 | tf_op jit(solution)/shard_map/all_to_all | solution.py:144
  404.7 16.1 %all-to-all-start.3 = ((bf16[64,2,512]{2,1,0:T(2,128)(2,1)}), bf16[64,2,512]{2,1,0:T(2,128)(2,1)S(1)}, u32[]{:S(2)}, u32[]{:S(2)}) async-start(bf16[64,2,512]{2,1,0:T(2,128)(2,1)} %reshape.900), calls=%async_computation.3 | async-start | bytes 262144 | tf_op jit(solution)/shard_map/all_to_all | solution.py:144
where the time goes:
time: 426 us; the launch traced here: 422 us
  blocking collectives  141 us (33%)
  local copies, waits for them, and re-layouts  124 us (29%)
  starting transfers between devices  49.2 us (12%)
  waiting for transfers between devices  40.4 us (9%)
  matrix products  32.7 us (8%)
  other arithmetic  31.7 us (7%)
    unnamed x1, blocking collectives  141 us
    gather x1, local copies, waits for them, and re-layouts, finish(): toeplitz = jnp.where(lower[None], taps[:, jnp.where(lower, differ, 0)], 0.0)  97.2 us
    dot_general x16, matrix products, one_mode(): inner = jnp.einsum('cij,csnj->csni', decay, inputs, precision=HIGH)  26.7 us
    all_to_all x3, starting transfers between devices, shards(): lax.all_to_all(shortened(flat), 'ctx', split_axis=1, concat_axis=0, tiled...  20.6 us
    all_to_all x1, starting transfers between devices, shards(): lax.all_to_all(grad_out, 'ctx', split_axis=0, concat_axis=1, tiled=True)  14.5 us
    all_to_all x3, waiting for transfers between devices, shards(): lax.all_to_all(shortened(flat), 'ctx', split_axis=1, concat_axis=0, tiled...  13.7 us
    unnamed x39, local copies, waits for them, and re-layouts  12.9 us
    dynamic_update_slice x16, local copies, waits for them, and re-layouts, mode_sums(): sums = lax.map(one_mode, (rate.T, jnp.moveaxis(previous, 3, 0)))  11.8 us
  transfers between devices with their start and end apart: 7, of which 5 were waited for; matrix products, arithmetic and copies ran while one was open for 27% of the time, Pallas kernels for 0%

commit v1 on v0

v1 whole, which is shorter than its diff:
```python
import functools
import math

import jax
import jax.numpy as jnp
from jax import lax
from jax.experimental import pallas as pl
from jax.experimental.pallas import tpu as pltpu
from jax.sharding import PartitionSpec as P

MODES = 16
LANES = 128
SUB = 8
HALF = 64
STEPS = 64
CHUNKS = 16
LOCAL = STEPS * CHUNKS
GROUP = 8
F32 = jnp.float32


def iota(shape, dim):
    return lax.broadcasted_iota(jnp.int32, shape, dim)


def mode_rows(table):
    wide = jnp.concatenate([table, jnp.zeros((HALF, LANES - MODES), F32)], axis=1)
    turned = jnp.concatenate([wide, wide], axis=0).T
    return turned[:MODES]


def to_steps(x, out_ref):
    for p in range(4):
        low = x[:, p * LANES : (p + 1) * LANES]
        high = x[:, (p + 4) * LANES : (p + 5) * LANES]
        out_ref[p * LANES : (p + 1) * LANES, :] = jnp.concatenate([low, high], axis=0).T


def step_rows(step):
    return pl.ds(step, SUB, stride=STEPS)


def summary_kernel(
    q_ref, k_ref, v_ref, g_ref, rate_ref, ut_ref, st_ref, sf_ref, sb_ref, msg_ref
):
    to_steps(k_ref[...].astype(F32) * v_ref[...].astype(F32), ut_ref)
    to_steps(g_ref[...].astype(F32) * q_ref[...].astype(F32), st_ref)
    rates = mode_rows(rate_ref[...])
    row = iota((SUB, LANES), 0)
    upper = iota((SUB, LANES), 1) >= HALF
    row_f = row.astype(F32)
    zero = jnp.zeros((SUB, LANES), F32)
    ends, adjoints, totals = [], [], []
    for half in range(2):
        modes = range(half * 8, half * 8 + 8)
        wide = [jnp.broadcast_to(rates[m : m + 1], (SUB, LANES)) for m in modes]
        factor = [jnp.exp(-r) for r in wide]

        def body(i, carry):
            state, total, back, direct = carry
            u = ut_ref[step_rows(i), :]
            s = st_ref[step_rows(i), :]
            sb = st_ref[step_rows(STEPS - 1 - i), :]
            state = [f * x + u for f, x in zip(factor, state)]
            total = [t + s * x for t, x in zip(total, state)]
            back = [f * x + sb for f, x in zip(factor, back)]
            return state, total, back, direct + s * u

        state, total, back, direct = lax.fori_loop(
            0, STEPS, body, ([zero] * 8, [zero] * 8, [zero] * 8, zero), unroll=8
        )
        for n, m in enumerate(modes):
            r = wide[n]
            decay = [jnp.exp(-(STEPS * d) * r) for d in (1, 2, 4)]
            half_decay = jnp.exp(-(STEPS * SUB) * r)
            scan = state[n]
            scan_b = back[n]
            for d, w in zip((1, 2, 4), decay):
                scan = scan + jnp.where(row >= d, w * pltpu.roll(scan, d, 0), 0.0)
                scan_b = scan_b + jnp.where(row < SUB - d, w * pltpu.roll(scan_b, SUB - d, 0), 0.0)
            last = jnp.broadcast_to(scan[SUB - 1 : SUB], (SUB, LANES))
            first = jnp.broadcast_to(scan_b[0:1], (SUB, LANES))
            last_other = pltpu.roll(last, HALF, 1)
            first_other = pltpu.roll(first, HALF, 1)
            start = jnp.where(row >= 1, pltpu.roll(scan, 1, 0), 0.0)
            start = start + jnp.where(upper, jnp.exp(-STEPS * row_f * r) * last_other, 0.0)
            start_b = jnp.where(row < SUB - 1, pltpu.roll(scan_b, SUB - 1, 0), 0.0)
            start_b = start_b + jnp.where(
                upper, 0.0, jnp.exp(-STEPS * (SUB - 1 - row_f) * r) * first_other
            )
            sf_ref[m] = start
            sb_ref[m] = start_b
            ends.append((last + half_decay * last_other)[0:1])
            adjoints.append((first + half_decay * first_other)[0:1])
            totals.append(
                jnp.sum(total[n] + start * factor[n] * back[n], axis=0, keepdims=True)
            )
    ends = jnp.concatenate(ends, axis=0)
    adjoints = jnp.concatenate(adjoints, axis=0)
    totals = jnp.concatenate(totals, axis=0)
    direct = jnp.broadcast_to(jnp.sum(direct, axis=0, keepdims=True), (MODES, LANES))
    totals = totals + pltpu.roll(totals, HALF, 1)
    direct = direct + pltpu.roll(direct, HALF, 1)
    lanes_up = iota((MODES, LANES), 1) >= HALF
    pair = jnp.where(lanes_up, ends, adjoints)
    sums = jnp.where(lanes_up, direct, totals)
    for j in range(GROUP):
        msg_ref[j, 0:MODES] = pair
        msg_ref[j, MODES : 2 * MODES] = sums


def combine(got_ref, rates, span, place):
    lanes_up = iota((MODES, LANES), 1) >= HALF
    rho = jnp.exp(-float(span) * rates)
    factor = jnp.exp(-rates)
    zero = jnp.zeros((MODES, LANES), F32)
    pairs = [got_ref[k, 0:MODES] for k in range(GROUP)]
    fwd, bwd = zero, zero
    enter_f, enter_b = zero, zero
    cross = zero
    sums = zero
    for k in range(GROUP):
        enter_f = jnp.where(place == k, fwd, enter_f)
        cross = cross + fwd * factor * pltpu.roll(pairs[k], HALF, 1)
        fwd = rho * fwd + pairs[k]
        sums = sums + got_ref[k, MODES : 2 * MODES]
    for k in reversed(range(GROUP)):
        enter_b = jnp.where(place == k, bwd, enter_b)
        bwd = rho * bwd + pairs[k]
    entering = jnp.where(lanes_up, enter_f, enter_b)
    joint = jnp.where(lanes_up, fwd, bwd)
    sums = sums + jnp.where(lanes_up, 0.0, pltpu.roll(cross, HALF, 1))
    return joint, sums, entering


def middle_kernel(place_ref, got_ref, rate_ref, msg_ref, enter_ref):
    rates = mode_rows(rate_ref[...])
    joint, sums, entering = combine(got_ref, rates, LOCAL, place_ref[0])
    enter_ref[...] = entering
    for j in range(GROUP):
        msg_ref[j, 0:MODES] = joint
        msg_ref[j, MODES : 2 * MODES] = sums


def final_kernel(
    place_ref,
    got_ref,
    enter_ref,
    sf_ref,
    sb_ref,
    ut_ref,
    st_ref,
    k_ref,
    v_ref,
    g_ref,
    rate_ref,
    weight_ref,
    gain_ref,
    skip_ref,
    gq_ref,
    gk_ref,
    gv_ref,
    gr_ref,
    gs_ref,
    mixed_ref,
    back_ref,
):
    rates = mode_rows(rate_ref[...])
    weights = mode_rows(weight_ref[...])
    joint, sums, outer = combine(got_ref, rates, LOCAL * GROUP, place_ref[1])
    lanes_up = iota((MODES, LANES), 1) >= HALF
    inner_place = place_ref[0]
    ahead = jnp.where(lanes_up, inner_place, GROUP - 1 - inner_place).astype(F32)
    entering = enter_ref[...] + jnp.exp(-(LOCAL * ahead) * rates) * outer
    turned = pltpu.roll(entering, HALF, 1)
    enter_f = jnp.where(lanes_up, entering, turned)
    enter_b = jnp.where(lanes_up, turned, entering)

    norm = 1.0 / math.sqrt(65536)
    tall = jnp.concatenate([sums, jnp.zeros((LANES - MODES, LANES), F32)], axis=0).T
    gr_ref[...] = gain_ref[...] * tall[:HALF, :MODES] * norm
    gs_ref[...] = sums[0:1, HALF:] * norm

    row = iota((SUB, LANES), 0)
    upper = iota((SUB, LANES), 1) >= HALF
    chunk = (row + jnp.where(upper, SUB, 0)).astype(F32)
    wide = [jnp.broadcast_to(rates[m : m + 1], (SUB, LANES)) for m in range(MODES)]
    factor = [jnp.exp(-r) for r in wide]
    weight = [jnp.broadcast_to(weights[m : m + 1], (SUB, LANES)) for m in range(MODES)]
    skip = jnp.broadcast_to(jnp.concatenate([skip_ref[...], skip_ref[...]], axis=1), (SUB, LANES))

    def added(terms):
        while len(terms) > 1:
            terms = [a + b for a, b in zip(terms[::2], terms[1::2])]
        return terms[0]

    def run(src_ref, dst_ref, start, flip):
        def body(i, state):
            rows = step_rows(STEPS - 1 - i if flip else i)
            x = src_ref[rows, :]
            state = [f * z + x for f, z in zip(factor, state)]
            dst_ref[rows, :] = added([w * z for w, z in zip(weight, state)]) + skip * x
            return state

        lax.fori_loop(0, STEPS, body, start, unroll=8)

    def lift(m, rows):
        return jnp.broadcast_to(rows[m : m + 1], (SUB, LANES))

    start_f = [
        sf_ref[m] + jnp.exp(-(STEPS * chunk) * wide[m]) * lift(m, enter_f) for m in range(MODES)
    ]
    run(ut_ref, mixed_ref, start_f, False)
    start_b = [
        sb_ref[m] + jnp.exp(-(STEPS * (CHUNKS - 1 - chunk)) * wide[m]) * lift(m, enter_b)
        for m in range(MODES)
    ]
    run(st_ref, back_ref, start_b, True)

    for p in range(4):
        rows = slice(p * LANES, (p + 1) * LANES)
        mixed = mixed_ref[rows, :].T
        back = back_ref[rows, :].T
        for b in range(2):
            cols = slice((p + 4 * b) * LANES, (p + 4 * b + 1) * LANES)
            chans = slice(b * HALF, (b + 1) * HALF)
            gq_ref[:, cols] = (g_ref[:, cols].astype(F32) * mixed[chans]).astype(jnp.bfloat16)
            gk_ref[:, cols] = (v_ref[:, cols].astype(F32) * back[chans]).astype(jnp.bfloat16)
            gv_ref[:, cols] = (k_ref[:, cols].astype(F32) * back[chans]).astype(jnp.bfloat16)


VMEM = pl.BlockSpec(memory_space=pltpu.VMEM)
SMEM = pl.BlockSpec(memory_space=pltpu.SMEM)
PARAMS = pltpu.CompilerParams(vmem_limit_bytes=32 * 1024 * 1024)
MESSAGE = jax.ShapeDtypeStruct((GROUP, 2 * MODES, LANES), F32)
STATES = jax.ShapeDtypeStruct((MODES, SUB, LANES), F32)
STEPPED = jax.ShapeDtypeStruct((STEPS * SUB, LANES), F32)


def shards(queries, keys, values, grad_out, residues, decay_rate, skip_gain):
    gain = jnp.sqrt(-jnp.expm1(-2.0 * decay_rate))
    weight = residues * gain
    me = lax.axis_index("ctx")
    place = jnp.stack([me % GROUP, me // GROUP]).astype(jnp.int32)
    near = [[z * GROUP + k for k in range(GROUP)] for z in range(GROUP)]
    far = [[z * GROUP + k for z in range(GROUP)] for k in range(GROUP)]

    ut, st, sf, sb, msg = pl.pallas_call(
        summary_kernel,
        out_shape=(STEPPED, STEPPED, STATES, STATES, MESSAGE),
        in_specs=[VMEM] * 5,
        out_specs=(VMEM,) * 5,
        compiler_params=PARAMS,
        name="summary",
    )(queries, keys, values, grad_out, decay_rate)
    got = lax.all_to_all(msg, "ctx", 0, 0, axis_index_groups=near)
    msg, enter = pl.pallas_call(
        middle_kernel,
        out_shape=(MESSAGE, jax.ShapeDtypeStruct((MODES, LANES), F32)),
        in_specs=[SMEM, VMEM, VMEM],
        out_specs=(VMEM,) * 2,
        compiler_params=PARAMS,
        name="middle",
    )(place, got, decay_rate)
    got = lax.all_to_all(msg, "ctx", 0, 0, axis_index_groups=far)
    wide = jax.ShapeDtypeStruct(queries.shape, jnp.bfloat16)
    grad_q, grad_k, grad_v, grad_res, grad_skip = pl.pallas_call(
        final_kernel,
        out_shape=(
            wide,
            wide,
            wide,
            jax.ShapeDtypeStruct((HALF, MODES), F32),
            jax.ShapeDtypeStruct((1, HALF), F32),
        ),
        in_specs=[SMEM] + [VMEM] * 13,
        out_specs=(VMEM,) * 5,
        scratch_shapes=[pltpu.VMEM((STEPS * SUB, LANES), F32)] * 2,
        compiler_params=PARAMS,
        name="final",
    )(
        place,
        got,
        enter,
        sf,
        sb,
        ut,
        st,
        keys,
        values,
        grad_out,
        decay_rate,
        weight,
        gain,
        skip_gain.reshape(1, HALF),
    )
    return (grad_q, grad_k, grad_v, grad_res, grad_skip.reshape(HALF))


def solution(mesh):
    in_specs = (
        P("tp", "ctx"),
        P("tp", "ctx"),
        P("tp", "ctx"),
        P("tp", "ctx"),
        P("tp", None),
        P("tp", None),
        P("tp"),
    )
    out_specs = (P("tp", "ctx"), P("tp", "ctx"), P("tp", "ctx"), P("tp", None), P("tp"))
    return jax.shard_map(shards, mesh=mesh, in_specs=in_specs, out_specs=out_specs, check_vma=False)
```

time: 426 us -> 45.4 us (0.11)
  blocking collectives: 141 us -> 0 us
  local copies, waits for them, and re-layouts: 124 us -> 5.81 us
  starting transfers between devices: 49.2 us -> 15.3 us
  matrix products: 32.7 us -> 0 us
  other arithmetic: 31.7 us -> 0.1 us
  waiting for transfers between devices: 40.4 us -> 15.6 us
  Pallas kernels: 0 us -> 7.46 us
    unnamed x1 -> x0, blocking collectives: 141 us -> none
    gather x1 -> x0, local copies, waits for them, and re-layouts: 97.2 us -> none  [finish(): toeplitz = jnp.where(lower[None], taps[:, jnp.where(lower, differ, 0)], 0.0)]
    all_to_all x7 -> x2, starting transfers between devices: 49.2 us -> 15.3 us  [the longest x1 10.4 us: shards(): got = lax.all_to_all(msg, 'ctx', 0, 0, axis_index_groups=far)]
    dot_general x27 -> x0, matrix products: 32.7 us -> none  [the longest x16 26.7 us: one_mode(): inner = jnp.einsum('cij,csnj->csni', decay, inputs, precision=HIGH)]
    all_to_all x7 -> x2, waiting for transfers between devices: 40.4 us -> 15.6 us  [the longest x1 8.94 us: shards(): got = lax.all_to_all(msg, 'ctx', 0, 0, axis_index_groups=far)]
    dynamic_update_slice x16 -> x0, local copies, waits for them, and re-layouts: 11.8 us -> none  [mode_sums(): sums = lax.map(one_mode, (rate.T, jnp.moveaxis(previous, 3, 0)))]
    exp x16 -> x0, other arithmetic: 10.4 us -> none  [one_mode(): jnp.exp(-rate_col[:, None] * leading[None])[:, None, None, :]]
    neg x16 -> x0, other arithmetic: 9.4 us -> none  [one_mode(): -rate_col[:, None, None] * safe[None]]
  transfers between devices with their start and end apart: 7 -> 2, of which waited for: 5 -> 2; matrix products, arithmetic and copies ran while one was open for 27% -> 0% of each run, Pallas kernels for 0% -> 0%
where the time goes in v1:
time: 45.4 us; the launch traced here: 45 us
  waiting for transfers between devices  15.6 us (34%)
  starting transfers between devices  15.3 us (34%)
  Pallas kernels  7.46 us (16%)
  local copies, waits for them, and re-layouts  5.81 us (13%)
  between operations  0.66 us (1%)
    all_to_all x1, starting transfers between devices, shards(): got = lax.all_to_all(msg, 'ctx', 0, 0, axis_index_groups=far)  10.4 us
    all_to_all x1, waiting for transfers between devices, shards(): got = lax.all_to_all(msg, 'ctx', 0, 0, axis_index_groups=far)  8.94 us
    all_to_all x1, waiting for transfers between devices, shards(): got = lax.all_to_all(msg, 'ctx', 0, 0, axis_index_groups=near)  6.71 us
    unnamed x21, local copies, waits for them, and re-layouts  5.81 us
    all_to_all x1, starting transfers between devices, shards(): got = lax.all_to_all(msg, 'ctx', 0, 0, axis_index_groups=near)  4.88 us
    pallas_call x1, Pallas kernels, shards(): pl.pallas_call(final_kernel, out_shape=(wide, wide, wide, jax.ShapeDtypeS...  3.49 us
    pallas_call x1, Pallas kernels, shards(): pl.pallas_call(summary_kernel, out_shape=(STEPPED, STEPPED, STATES, STATE...  2.6 us
    pallas_call x1, Pallas kernels, shards(): pl.pallas_call(middle_kernel, out_shape=(MESSAGE, jax.ShapeDtypeStruct((M...  1.37 us
  transfers between devices with their start and end apart: 2, of which 2 were waited for; matrix products, arithmetic and copies ran while one was open for 0% of the time, Pallas kernels for 0%

profile of v1, /device:TPU:6, one launch (start us, length us, event | category | flops | bytes accessed | tf_op | source)
XLA Modules:
  0.0 45.0 jit_solution(11341968269409839883)
XLA Ops:
  0.6 0.8 %copy.18.rate_ref = f32[64,16]{1,0:T(8,128)S(1)} copy(f32[64,16]{0,1:T(8,128)} %param.12) | data formatting | bytes 8192 | tf_op args[5]
  1.4 0.0 copy-start
  1.4 0.9 %copy-done = bf16[64,1024]{1,0:T(8,128)(2,1)S(1)} copy-done((bf16[64,1024]{1,0:T(8,128)(2,1)S(1)}, bf16[64,1024]{1,0:T(8,128)(2,1)}, u32[]{:S(2)}) %copy-start) | copy-done | bytes 131096
  2.3 0.0 copy-start.2
  2.3 0.9 %copy-done.2 = bf16[64,1024]{1,0:T(8,128)(2,1)S(1)} copy-done((bf16[64,1024]{1,0:T(8,128)(2,1)S(1)}, bf16[64,1024]{1,0:T(8,128)(2,1)}, u32[]{:S(2)}) %copy-start.2) | copy-done | bytes 131096
  3.2 0.0 copy-start.4
  3.2 0.9 %copy-done.4 = bf16[64,1024]{1,0:T(8,128)(2,1)S(1)} copy-done((bf16[64,1024]{1,0:T(8,128)(2,1)S(1)}, bf16[64,1024]{1,0:T(8,128)(2,1)}, u32[]{:S(2)}) %copy-start.4) | copy-done | bytes 131096
  4.1 0.0 copy-start.6
  4.1 0.9 %copy-done.6 = bf16[64,1024]{1,0:T(8,128)(2,1)S(1)} copy-done((bf16[64,1024]{1,0:T(8,128)(2,1)S(1)}, bf16[64,1024]{1,0:T(8,128)(2,1)}, u32[]{:S(2)}) %copy-start.6) | copy-done | bytes 131096
  5.0 2.6 %summary.1 = (f32[512,128]{1,0:T(8,128)S(1)}, f32[512,128]{1,0:T(8,128)S(1)}, f32[16,8,128]{2,1,0:T(8,128)S(1)}, f32[16,8,128]{2,1,0:T(8,128)S(1)}, f32[8,32,128]{2,1,0:T(8,128)}) custom-call(bf16[64,1024]{1,0:T(8,128)(2,1)S(1)} %copy-done.6, bf16[64,1024]{1,0:T(8,128)(2,1)S(1)} %copy-done, bf16[64,1024]{1,0:T(8,128)(2,1)S(1)} %copy-done.2, ...), custom_call_target="tpu_custom_call" | custom-call | tf_op jit(solution)/shard_map/summary/pallas_call | solution.py:248
  7.6 4.9 %all-to-all-start = ((f32[8,32,128]{2,1,0:T(8,128)}), f32[8,32,128]{2,1,0:T(8,128)S(1)}, u32[]{:S(2)}, u32[]{:S(2)}) async-start(f32[8,32,128]{2,1,0:T(8,128)} %get-tuple-element.17), calls=%async_computation | async-start | bytes 262144 | tf_op jit(solution)/shard_map/all_to_all | solution.py:256
  12.5 0.1 pad_add_fusion.place_ref
  12.6 6.7 %all-to-all-done.got_ref = f32[8,32,128]{2,1,0:T(8,128)S(1)} async-done(((f32[8,32,128]{2,1,0:T(8,128)}), f32[8,32,128]{2,1,0:T(8,128)S(1)}, u32[]{:S(2)}, u32[]{:S(2)}) %all-to-all-start) | async-done | bytes 131104 | tf_op jit(solution)/shard_map/all_to_all | solution.py:256
  19.3 0.0 copy-start.8
  19.3 1.4 %middle.1 = (f32[8,32,128]{2,1,0:T(8,128)}, f32[16,128]{1,0:T(8,128)S(1)}) custom-call(s32[2]{0:T(128)S(1)} %pad_add_fusion.place_ref, f32[8,32,128]{2,1,0:T(8,128)S(1)} %all-to-all-done.got_ref, f32[64,16]{1,0:T(8,128)S(1)} %copy.18.rate_ref), custom_call_target="tpu_custom_call" | custom-call | tf_op jit(solution)/shard_map/middle/pallas_call | solution.py:257
  20.7 0.0 copy-start.3
  20.7 0.0 copy-start.5
  20.7 10.4 %all-to-all-start.1 = ((f32[8,32,128]{2,1,0:T(8,128)}), f32[8,32,128]{2,1,0:T(8,128)S(1)}, u32[]{:S(2)}, u32[]{:S(2)}) async-start(f32[8,32,128]{2,1,0:T(8,128)} %get-tuple-element.18), calls=%async_computation.1 | async-start | bytes 262144 | tf_op jit(solution)/shard_map/all_to_all | solution.py:265
  31.1 0.0 copy-done.8
  31.1 0.0 copy-start.1
  31.1 0.1 copy.22
  31.3 8.9 %all-to-all-done.1.got_ref = f32[8,32,128]{2,1,0:T(8,128)S(1)} async-done(((f32[8,32,128]{2,1,0:T(8,128)}), f32[8,32,128]{2,1,0:T(8,128)S(1)}, u32[]{:S(2)}, u32[]{:S(2)}) %all-to-all-start.1) | async-done | bytes 131104 | tf_op jit(solution)/shard_map/all_to_all | solution.py:265
  40.2 0.0 copy-start.7
  40.2 0.0 copy-done.3
  40.2 0.0 copy-done.5
  40.2 0.0 copy-done.1
  40.2 0.6 %copy-done.7 = f32[64]{0:T(128)S(1)} copy-done((f32[64]{0:T(128)S(1)}, f32[64]{0:T(128)}, u32[]{:S(2)}) %copy-start.7) | copy-done | bytes 280
  40.9 3.5 %final.1 = (bf16[64,1024]{1,0:T(8,128)(2,1)}, bf16[64,1024]{1,0:T(8,128)(2,1)}, bf16[64,1024]{1,0:T(8,128)(2,1)}, f32[64,16]{1,0:T(8,128)S(1)}, f32[1,64]{1,0:T(1,128)}) custom-call(s32[2]{0:T(128)S(1)} %pad_add_fusion.place_ref, f32[8,32,128]{2,1,0:T(8,128)S(1)} %all-to-all-done.1.got_ref, f32[16,128]{1,0:T(8,128)S(1)} %get-tuple-element.19.enter_ref, ...), custom_call_target="tpu_custom_call" | custom-call | tf_op jit(solution)/shard_map/final/pallas_call | solution.py:267
  44.3 0.7 %copy.24 = f32[64,16]{0,1:T(8,128)} copy(f32[64,16]{1,0:T(8,128)S(1)} %get-tuple-element.37) | data formatting | bytes 8192
  (1 shorter events, 0.0 us)
Async XLA Ops:
  1.4 0.9 %copy-start = (bf16[64,1024]{1,0:T(8,128)(2,1)S(1)}, bf16[64,1024]{1,0:T(8,128)(2,1)}, u32[]{:S(2)}) copy-start(bf16[64,1024]{1,0:T(8,128)(2,1)} %k_ref.3) | copy-start | bytes 393220
  2.3 0.9 %copy-start.2 = (bf16[64,1024]{1,0:T(8,128)(2,1)S(1)}, bf16[64,1024]{1,0:T(8,128)(2,1)}, u32[]{:S(2)}) copy-start(bf16[64,1024]{1,0:T(8,128)(2,1)} %v_ref.3) | copy-start | bytes 393220
  3.2 0.9 %copy-start.4 = (bf16[64,1024]{1,0:T(8,128)(2,1)S(1)}, bf16[64,1024]{1,0:T(8,128)(2,1)}, u32[]{:S(2)}) copy-start(bf16[64,1024]{1,0:T(8,128)(2,1)} %g_ref.3) | copy-start | bytes 393220
  4.1 0.9 %copy-start.6 = (bf16[64,1024]{1,0:T(8,128)(2,1)S(1)}, bf16[64,1024]{1,0:T(8,128)(2,1)}, u32[]{:S(2)}) copy-start(bf16[64,1024]{1,0:T(8,128)(2,1)} %q_ref.1) | copy-start | bytes 393220
  7.6 11.7 %all-to-all-start = ((f32[8,32,128]{2,1,0:T(8,128)}), f32[8,32,128]{2,1,0:T(8,128)S(1)}, u32[]{:S(2)}, u32[]{:S(2)}) async-start(f32[8,32,128]{2,1,0:T(8,128)} %get-tuple-element.17), calls=%async_computation | async-start | bytes 262144 | tf_op jit(solution)/shard_map/all_to_all | solution.py:256
  19.3 11.8 %copy-start.8 = (f32[64,16]{0,1:T(8,128)S(1)}, f32[64,16]{0,1:T(8,128)}, u32[]{:S(2)}) copy-start(f32[64,16]{0,1:T(8,128)} %param.11) | copy-start | bytes 12292
  20.7 19.5 %copy-start.3 = (bf16[64,1024]{1,0:T(8,128)(2,1)S(1)}, bf16[64,1024]{1,0:T(8,128)(2,1)}, u32[]{:S(2)}) copy-start(bf16[64,1024]{1,0:T(8,128)(2,1)} %v_ref.3) | copy-start | bytes 393220
  20.7 19.5 %copy-start.5 = (bf16[64,1024]{1,0:T(8,128)(2,1)S(1)}, bf16[64,1024]{1,0:T(8,128)(2,1)}, u32[]{:S(2)}) copy-start(bf16[64,1024]{1,0:T(8,128)(2,1)} %g_ref.3) | copy-start | bytes 393220
  20.7 19.5 %all-to-all-start.1 = ((f32[8,32,128]{2,1,0:T(8,128)}), f32[8,32,128]{2,1,0:T(8,128)S(1)}, u32[]{:S(2)}, u32[]{:S(2)}) async-start(f32[8,32,128]{2,1,0:T(8,128)} %get-tuple-element.18), calls=%async_computation.1 | async-start | bytes 262144 | tf_op jit(solution)/shard_map/all_to_all | solution.py:265
  31.1 9.1 %copy-start.1 = (bf16[64,1024]{1,0:T(8,128)(2,1)S(1)}, bf16[64,1024]{1,0:T(8,128)(2,1)}, u32[]{:S(2)}) copy-start(bf16[64,1024]{1,0:T(8,128)(2,1)} %k_ref.3) | copy-start | bytes 393220
  40.2 0.7 %copy-start.7 = (f32[64]{0:T(128)S(1)}, f32[64]{0:T(128)}, u32[]{:S(2)}) copy-start(f32[64]{0:T(128)} %param.13) | copy-start | bytes 772

commit v2 on v1

v2 whole, which is shorter than its diff:
```python
import math

import jax
import jax.numpy as jnp
from jax import lax
from jax.experimental import pallas as pl
from jax.experimental.pallas import tpu as pltpu
from jax.sharding import PartitionSpec as P

MODES = 16
LANES = 128
SUB = 8
HALF = 64
STEPS = 64
PITCH = STEPS + 1
CHUNKS = 16
LOCAL = STEPS * CHUNKS
GROUP = 8
F32 = jnp.float32


def iota(shape, dim):
    return lax.broadcasted_iota(jnp.int32, shape, dim)


def twice(rows):
    return jnp.concatenate([rows, rows], axis=1)


def lift(rows, m):
    return jnp.broadcast_to(rows[m : m + 1], (SUB, LANES))


def to_steps(x, out_ref):
    for p in range(4):
        low = x[:, p * LANES : (p + 1) * LANES]
        high = x[:, (p + 4) * LANES : (p + 5) * LANES]
        turned = jnp.concatenate([low, high], axis=0).T
        for q in range(2):
            first = (2 * p + q) * PITCH
            out_ref[first : first + STEPS, :] = turned[q * STEPS : (q + 1) * STEPS]


def from_steps(ref, p):
    first = 2 * p * PITCH
    parts = [ref[first : first + STEPS, :], ref[first + PITCH : first + PITCH + STEPS, :]]
    return jnp.concatenate(parts, axis=0).T


def step_rows(step):
    return pl.ds(step, SUB, stride=PITCH)


def summary_kernel(
    q_any, k_any, v_any, g_any, rate_any,
    ut_any, st_any, sf_any, xb_any, msg_any,
    q_ref, k_ref, v_ref, g_ref, rate_ref, ut_ref, st_ref, sf_ref, xb_ref, msg_ref,
    row_ref, decay_ref, in_sems, out_sems, msg_sems,
):
    pairs = ((rate_any, rate_ref), (k_any, k_ref), (v_any, v_ref), (g_any, g_ref), (q_any, q_ref))
    copies = [pltpu.make_async_copy(a, b, in_sems.at[n]) for n, (a, b) in enumerate(pairs)]
    for copy in copies:
        copy.start()

    copies[0].wait()
    rates = twice(rate_ref[...])
    row_ref[0] = rates
    row_ref[1] = jnp.exp(-rates)
    row_ref[2] = jnp.exp(-float(STEPS * SUB) * rates)
    row = iota((SUB, LANES), 0)
    upper = iota((SUB, LANES), 1) >= HALF
    row_f = row.astype(F32)
    chunk = jnp.where(upper, row_f + SUB, row_f)
    for m in range(MODES):
        r = row_ref[0, m : m + 1, :]
        for n, d in enumerate((1, 2, 4)):
            decay_ref[m, n] = jnp.where(row >= d, jnp.exp(-float(STEPS * d) * r), 0.0)
        decay_ref[m, 3] = jnp.where(upper, jnp.exp(-(STEPS * row_f) * r), 0.0)
        decay_ref[m, 4] = jnp.exp(-(STEPS * chunk) * r)

    copies[1].wait()
    copies[2].wait()
    to_steps(k_ref[...].astype(F32) * v_ref[...].astype(F32), ut_ref)
    copy_u = pltpu.make_async_copy(ut_ref, ut_any, out_sems.at[0])
    copy_u.start()
    copies[3].wait()
    copies[4].wait()
    to_steps(g_ref[...].astype(F32) * q_ref[...].astype(F32), st_ref)
    copy_s = pltpu.make_async_copy(st_ref, st_any, out_sems.at[1])
    copy_s.start()

    zero = jnp.zeros((SUB, LANES), F32)
    ends, adjoints, totals = [], [], []
    for half in range(2):
        modes = range(half * 8, half * 8 + 8)
        factor = [jnp.broadcast_to(row_ref[1, m : m + 1, :], (SUB, LANES)) for m in modes]

        def body(i, carry):
            state, total, back, direct = carry
            u = ut_ref[step_rows(i), :]
            s = st_ref[step_rows(i), :]
            sb = st_ref[step_rows(STEPS - 1 - i), :]
            state = [f * x + u for f, x in zip(factor, state)]
            total = [t + s * x for t, x in zip(total, state)]
            back = [f * x + sb for f, x in zip(factor, back)]
            if half == 0:
                direct = direct + s * u
            return state, total, back, direct

        if half == 0:
            direct = zero
        state, total, back, direct = lax.fori_loop(
            0, STEPS, body, ([zero] * 8, [zero] * 8, [zero] * 8, direct), unroll=8
        )
        for n, m in enumerate(modes):
            scan = state[n]
            for j, d in enumerate((1, 2, 4)):
                scan = scan + decay_ref[m, j] * pltpu.roll(scan, d, 0)
            last = scan[SUB - 1 : SUB]
            last_other = pltpu.roll(last, HALF, 1)
            start = jnp.where(row >= 1, pltpu.roll(scan, 1, 0), 0.0)
            start = start + decay_ref[m, 3] * last_other
            sf_ref[m] = start
            xb_ref[m] = back[n]
            ends.append(last + row_ref[2, m : m + 1, :] * last_other)
            adjoints.append(jnp.sum(decay_ref[m, 4] * back[n], axis=0, keepdims=True))
            totals.append(
                jnp.sum(total[n] + start * factor[n] * back[n], axis=0, keepdims=True)
            )
    copy_sf = pltpu.make_async_copy(sf_ref, sf_any, out_sems.at[2])
    copy_sf.start()
    copy_xb = pltpu.make_async_copy(xb_ref, xb_any, out_sems.at[3])
    copy_xb.start()
    ends = jnp.concatenate(ends, axis=0)
    adjoints = jnp.concatenate(adjoints, axis=0)
    totals = jnp.concatenate(totals, axis=0)
    direct = jnp.broadcast_to(jnp.sum(direct, axis=0, keepdims=True), (MODES, LANES))
    adjoints = adjoints + pltpu.roll(adjoints, HALF, 1)
    totals = totals + pltpu.roll(totals, HALF, 1)
    direct = direct + pltpu.roll(direct, HALF, 1)
    lanes_up = iota((MODES, LANES), 1) >= HALF
    msg_ref[0:MODES] = jnp.where(lanes_up, ends, adjoints)
    msg_ref[MODES : 2 * MODES] = jnp.where(lanes_up, direct, totals)
    sends = [
        pltpu.make_async_copy(msg_ref, msg_any.at[j], msg_sems.at[j]) for j in range(GROUP)
    ]
    for copy in sends:
        copy.start()
    for copy in [copy_u, copy_s, copy_sf, copy_xb] + sends:
        copy.wait()


def local_kernel(
    place_ref, ut_ref, st_ref, sf_ref, xb_ref, rate_ref, weight_ref, gain_ref, skip_ref,
    mixed_ref, back_ref, zf_ref, zb_ref, table_ref, near_ref, far_ref,
):
    rates = twice(rate_ref[...])
    weights = twice(weight_ref[...])
    skip_row = skip_ref[...]
    skip = jnp.broadcast_to(jnp.concatenate([skip_row, skip_row], axis=1), (SUB, LANES))
    wide = [lift(rates, m) for m in range(MODES)]
    factor = [jnp.exp(-r) for r in wide]
    weight = [lift(weights, m) for m in range(MODES)]

    def added(terms):
        while len(terms) > 1:
            terms = [a + b for a, b in zip(terms[::2], terms[1::2])]
        return terms[0]

    def run(src_ref, dst_ref, start, flip):
        def body(i, state):
            rows = step_rows(STEPS - 1 - i if flip else i)
            x = src_ref[rows, :]
            state = [f * z + x for f, z in zip(factor, state)]
            dst_ref[rows, :] = added([w * z for w, z in zip(weight, state)]) + skip * x
            return state

        lax.fori_loop(0, STEPS, body, start, unroll=8)

    row = iota((SUB, LANES), 0)
    upper = iota((SUB, LANES), 1) >= HALF
    run(ut_ref, mixed_ref, [sf_ref[m] for m in range(MODES)], False)
    start_b = []
    for m in range(MODES):
        scan = xb_ref[m]
        for d in (1, 2, 4):
            decay = jnp.where(row < SUB - d, jnp.exp(-float(STEPS * d) * wide[m]), 0.0)
            scan = scan + decay * pltpu.roll(scan, SUB - d, 0)
        first_other = pltpu.roll(lift(scan, 0), HALF, 1)
        start = jnp.where(row < SUB - 1, pltpu.roll(scan, SUB - 1, 0), 0.0)
        decay = jnp.exp(-(STEPS * (SUB - 1 - row).astype(F32)) * wide[m])
        start_b.append(start + jnp.where(upper, 0.0, decay * first_other))
    run(st_ref, back_ref, start_b, True)

    chunk = (row + jnp.where(upper, SUB, 0)).astype(F32)
    for m in range(MODES):
        zf_ref[m] = weight[m] * jnp.exp(-(STEPS * chunk + 1.0) * wide[m])
        zb_ref[m] = weight[m] * jnp.exp(-(STEPS * (CHUNKS - 1 - chunk) + 1.0) * wide[m])
    lanes_up = iota((MODES, LANES), 1) >= HALF
    place = place_ref[0]
    ahead = jnp.where(lanes_up, place, GROUP - 1 - place).astype(F32)
    for k in range(GROUP):
        near_ref[k] = jnp.broadcast_to((place == k).astype(F32), (MODES, LANES))
        far_ref[k] = jnp.broadcast_to((place_ref[1] == k).astype(F32), (MODES, LANES))
    table_ref[0] = jnp.exp(-rates)
    table_ref[1] = jnp.exp(-float(LOCAL) * rates)
    table_ref[2] = jnp.exp(-float(LOCAL * GROUP) * rates)
    table_ref[3] = jnp.exp(-(LOCAL * ahead) * rates)
    norm = 1.0 / math.sqrt(65536)
    table_ref[4] = jnp.where(lanes_up, norm, twice(gain_ref[...]) * norm)


def combine(got_ref, factor, rho, chosen_ref):
    lanes_up = iota((MODES, LANES), 1) >= HALF
    zero = jnp.zeros((MODES, LANES), F32)
    pairs = [got_ref[k, 0:MODES] for k in range(GROUP)]
    fwd, bwd = zero, zero
    enter_f, enter_b = zero, zero
    cross = zero
    sums = zero
    for k in range(GROUP):
        enter_f = enter_f + chosen_ref[k] * fwd
        cross = cross + fwd * pltpu.roll(pairs[k], HALF, 1)
        fwd = rho * fwd + pairs[k]
        sums = sums + got_ref[k, MODES : 2 * MODES]
    for k in reversed(range(GROUP)):
        enter_b = enter_b + chosen_ref[k] * bwd
        bwd = rho * bwd + pairs[k]
    entering = jnp.where(lanes_up, enter_f, enter_b)
    joint = jnp.where(lanes_up, fwd, bwd)
    sums = sums + jnp.where(lanes_up, 0.0, pltpu.roll(factor * cross, HALF, 1))
    return joint, sums, entering


def middle_kernel(got_ref, table_ref, near_ref, msg_ref, enter_ref):
    joint, sums, entering = combine(got_ref, table_ref[0], table_ref[1], near_ref)
    enter_ref[...] = entering
    for j in range(GROUP):
        msg_ref[j, 0:MODES] = joint
        msg_ref[j, MODES : 2 * MODES] = sums


def final_kernel(
    got_ref, enter_ref, table_ref, far_ref, zf_ref, zb_ref, mixed_ref, back_ref,
    k_ref, v_ref, g_ref,
    gq_any, gk_any, gv_any, gr_ref, gs_ref,
    gq_ref, gk_ref, gv_ref, fwd_ref, bwd_ref, sems,
):
    factors = table_ref[0]
    joint, sums, outer = combine(got_ref, factors, table_ref[2], far_ref)
    lanes_up = iota((MODES, LANES), 1) >= HALF
    entering = enter_ref[...] + table_ref[3] * outer
    turned = pltpu.roll(entering, HALF, 1)
    enter_f = jnp.where(lanes_up, entering, turned)
    enter_b = jnp.where(lanes_up, turned, entering)
    scaled = sums * table_ref[4]
    gr_ref[...] = scaled[:, :HALF]
    gs_ref[...] = scaled[0:1, HALF:]

    factor = [lift(factors, m) for m in range(MODES)]

    def added(terms):
        while len(terms) > 1:
            terms = [a + b for a, b in zip(terms[::2], terms[1::2])]
        return terms[0]

    def run(src_ref, dst_ref, start, flip):
        def body(i, z):
            rows = step_rows(STEPS - 1 - i if flip else i)
            dst_ref[rows, :] = src_ref[rows, :] + added(z)
            return [f * x for f, x in zip(factor, z)]

        lax.fori_loop(0, STEPS, body, start, unroll=8)

    run(mixed_ref, fwd_ref, [zf_ref[m] * lift(enter_f, m) for m in range(MODES)], False)
    for p in range(4):
        turned = from_steps(fwd_ref, p)
        for b in range(2):
            cols = slice((p + 4 * b) * LANES, (p + 4 * b + 1) * LANES)
            part = turned[b * HALF : (b + 1) * HALF]
            gq_ref[:, cols] = (g_ref[:, cols].astype(F32) * part).astype(jnp.bfloat16)
    copy_q = pltpu.make_async_copy(gq_ref, gq_any, sems.at[0])
    copy_q.start()
    run(back_ref, bwd_ref, [zb_ref[m] * lift(enter_b, m) for m in range(MODES)], True)
    for p in range(4):
        turned = from_steps(bwd_ref, p)
        for b in range(2):
            cols = slice((p + 4 * b) * LANES, (p + 4 * b + 1) * LANES)
            part = turned[b * HALF : (b + 1) * HALF]
            gk_ref[:, cols] = (v_ref[:, cols].astype(F32) * part).astype(jnp.bfloat16)
            gv_ref[:, cols] = (k_ref[:, cols].astype(F32) * part).astype(jnp.bfloat16)
    copy_k = pltpu.make_async_copy(gk_ref, gk_any, sems.at[1])
    copy_v = pltpu.make_async_copy(gv_ref, gv_any, sems.at[2])
    copy_k.start()
    copy_v.start()
    copy_q.wait()
    copy_k.wait()
    copy_v.wait()


VMEM = pl.BlockSpec(memory_space=pltpu.VMEM)
SMEM = pl.BlockSpec(memory_space=pltpu.SMEM)
ANY = pl.BlockSpec(memory_space=pl.ANY)
PARAMS = pltpu.CompilerParams(vmem_limit_bytes=32 * 1024 * 1024)
MESSAGE = jax.ShapeDtypeStruct((GROUP, 2 * MODES, LANES), F32)
STATES = jax.ShapeDtypeStruct((MODES, SUB, LANES), F32)
STEPPED = jax.ShapeDtypeStruct((PITCH * SUB, LANES), F32)


def shards(queries, keys, values, grad_out, residues, decay_rate, skip_gain):
    rate = decay_rate.T
    gain = jnp.sqrt(-jnp.expm1(-2.0 * rate))
    weight = residues.T * gain
    me = lax.axis_index("ctx")
    place = jnp.stack([me % GROUP, me // GROUP]).astype(jnp.int32)
    near = [[z * GROUP + k for k in range(GROUP)] for z in range(GROUP)]
    far = [[z * GROUP + k for z in range(GROUP)] for k in range(GROUP)]
    wide = jax.ShapeDtypeStruct(queries.shape, jnp.bfloat16)
    held = pltpu.VMEM(queries.shape, jnp.bfloat16)

    stepped = pltpu.VMEM(STEPPED.shape, F32)
    states = pltpu.VMEM(STATES.shape, F32)
    ut, st, sf, xb, msg = pl.pallas_call(
        summary_kernel,
        out_shape=(STEPPED, STEPPED, STATES, STATES, MESSAGE),
        in_specs=[ANY] * 5,
        out_specs=(ANY,) * 5,
        scratch_shapes=[held] * 4
        + [pltpu.VMEM((MODES, HALF), F32), stepped, stepped, states, states]
        + [pltpu.VMEM(MESSAGE.shape[1:], F32), pltpu.VMEM((3, MODES, LANES), F32)]
        + [pltpu.VMEM((MODES, 5, SUB, LANES), F32)]
        + [pltpu.SemaphoreType.DMA((n,)) for n in (5, 4, GROUP)],
        name="summary",
    )(queries, keys, values, grad_out, rate)
    got = lax.all_to_all(msg, "ctx", 0, 0, axis_index_groups=near)
    mixed, back, zf, zb, table, near_at, far_at = pl.pallas_call(
        local_kernel,
        out_shape=(STEPPED, STEPPED, STATES, STATES)
        + tuple(jax.ShapeDtypeStruct((n, MODES, LANES), F32) for n in (5, GROUP, GROUP)),
        in_specs=[SMEM] + [VMEM] * 8,
        out_specs=(VMEM,) * 7,
        compiler_params=PARAMS,
        cost_estimate=pl.CostEstimate(
            flops=8 * STEPS * MODES * SUB * LANES, bytes_accessed=1 << 20, transcendentals=0
        ),
        name="local",
    )(place, ut, st, sf, xb, rate, weight, gain, skip_gain.reshape(1, HALF))
    msg, enter = pl.pallas_call(
        middle_kernel,
        out_shape=(MESSAGE, jax.ShapeDtypeStruct((MODES, LANES), F32)),
        in_specs=[VMEM] * 3,
        out_specs=(VMEM,) * 2,
        compiler_params=PARAMS,
        name="middle",
    )(got, table, near_at)
    got = lax.all_to_all(msg, "ctx", 0, 0, axis_index_groups=far)
    grad_q, grad_k, grad_v, grad_res, grad_skip = pl.pallas_call(
        final_kernel,
        out_shape=(
            wide,
            wide,
            wide,
            jax.ShapeDtypeStruct((MODES, HALF), F32),
            jax.ShapeDtypeStruct((1, HALF), F32),
        ),
        in_specs=[VMEM] * 11,
        out_specs=(ANY,) * 3 + (VMEM,) * 2,
        scratch_shapes=[held] * 3 + [stepped, stepped, pltpu.SemaphoreType.DMA((3,))],
        compiler_params=PARAMS,
        name="final",
    )(got, enter, table, far_at, zf, zb, mixed, back, keys, values, grad_out)
    return (grad_q, grad_k, grad_v, grad_res.T, grad_skip.reshape(HALF))


def solution(mesh):
    in_specs = (
        P("tp", "ctx"),
        P("tp", "ctx"),
        P("tp", "ctx"),
        P("tp", "ctx"),
        P("tp", None),
        P("tp", None),
        P("tp"),
    )
    out_specs = (P("tp", "ctx"), P("tp", "ctx"), P("tp", "ctx"), P("tp", None), P("tp"))
    return jax.shard_map(shards, mesh=mesh, in_specs=in_specs, out_specs=out_specs, check_vma=False)
```

time: 45.4 us -> 39.1 us (0.86)
  the two profiles are of different devices: /device:TPU:6 before, /device:TPU:56 now
where the time goes in v2:
time: 39.1 us; the launch traced here: 38.7 us
  blocking collectives  19.6 us (50%)
  Pallas kernels  7.96 us (20%)
  starting transfers between devices  6.37 us (16%)
  local copies, waits for them, and re-layouts  3.92 us (10%)
  between operations  0.69 us (2%)
    all_to_all x1, blocking collectives, shards(): got = lax.all_to_all(msg, 'ctx', 0, 0, axis_index_groups=far)  19.6 us
    all_to_all x1, starting transfers between devices, shards(): got = lax.all_to_all(msg, 'ctx', 0, 0, axis_index_groups=near)  6.37 us
    unnamed x20, local copies, waits for them, and re-layouts  3.92 us
    pallas_call x1, Pallas kernels, shards(): pl.pallas_call(summary_kernel, out_shape=(STEPPED, STEPPED, STATES, STATE...  3.33 us
    pallas_call x1, Pallas kernels, shards(): pl.pallas_call(final_kernel, out_shape=(wide, wide, wide, jax.ShapeDtypeS...  2.48 us
    pallas_call x1, Pallas kernels, shards(): pl.pallas_call(local_kernel, out_shape=(STEPPED, STEPPED, STATES, STATES)...  1.99 us
  transfers between devices with their start and end apart: 1, of which 0 were waited for; matrix products, arithmetic and copies ran while one was open for 0% of the time, Pallas kernels for 5%

profile of v2, /device:TPU:56, one launch (start us, length us, event | category | flops | bytes accessed | tf_op | source)
XLA Modules:
  0.0 38.7 jit_solution(10803491970957334291)
XLA Ops:
  0.6 3.3 %summary.1 = (f32[520,128]{1,0:T(8,128)}, f32[520,128]{1,0:T(8,128)}, f32[16,8,128]{2,1,0:T(8,128)}, f32[16,8,128]{2,1,0:T(8,128)}, f32[8,32,128]{2,1,0:T(8,128)}) custom-call(bf16[64,1024]{1,0:T(8,128)(2,1)} %q_any.1, bf16[64,1024]{1,0:T(8,128)(2,1)} %k_ref.1, bf16[64,1024]{1,0:T(8,128)(2,1)} %v_ref.1, bf16[64,1024]{1,0:T(8,128)(2,1)} %g_ref.1, ...), custom_call_target="tpu_custom_call" | custom-call | tf_op jit(solution)/shard_map/summary/pallas_call | solution.py:323
  4.0 0.0 copy-start.3
  4.0 6.4 %all-to-all-start = ((f32[8,32,128]{2,1,0:T(8,128)}), f32[8,32,128]{2,1,0:T(8,128)S(1)}, u32[]{:S(2)}, u32[]{:S(2)}) async-start(f32[8,32,128]{2,1,0:T(8,128)} %get-tuple-element.24), calls=%async_computation | async-start | bytes 262144 | tf_op jit(solution)/shard_map/all_to_all | solution.py:335
  10.4 0.0 copy-start.9
  10.4 0.0 copy-start.5
  10.4 0.1 pad_add_fusion.place_ref
  10.4 0.6 %copy-done.9 = f32[64,16]{0,1:T(8,128)S(1)} copy-done((f32[64,16]{0,1:T(8,128)S(1)}, f32[64,16]{0,1:T(8,128)}, u32[]{:S(2)}) %copy-start.9) | copy-done | bytes 4120
  11.0 0.0 copy-done.5
  11.1 0.0 copy-start.8
  11.1 0.0 copy-done.3
  11.1 0.6 %copy-done.8 = f32[64]{0:T(128)S(1)} copy-done((f32[64]{0:T(128)S(1)}, f32[64]{0:T(128)}, u32[]{:S(2)}) %copy-start.8) | copy-done | bytes 280
  11.7 0.0 copy-start.4
  11.7 0.9 %copy-done.4 = f32[520,128]{1,0:T(8,128)S(1)} copy-done((f32[520,128]{1,0:T(8,128)S(1)}, f32[520,128]{1,0:T(8,128)}, u32[]{:S(2)}) %copy-start.4) | copy-done | bytes 266264
  12.7 0.0 copy-start.6
  12.7 0.8 %copy-done.6 = f32[16,8,128]{2,1,0:T(8,128)S(1)} copy-done((f32[16,8,128]{2,1,0:T(8,128)S(1)}, f32[16,8,128]{2,1,0:T(8,128)}, u32[]{:S(2)}) %copy-start.6) | copy-done | bytes 65560
  13.5 0.0 copy-start.7
  13.5 0.8 %copy-done.7 = f32[16,8,128]{2,1,0:T(8,128)S(1)} copy-done((f32[16,8,128]{2,1,0:T(8,128)S(1)}, f32[16,8,128]{2,1,0:T(8,128)}, u32[]{:S(2)}) %copy-start.7) | copy-done | bytes 65560
  14.4 2.0 %local.1 = (f32[520,128]{1,0:T(8,128)S(1)}, f32[520,128]{1,0:T(8,128)S(1)}, f32[16,8,128]{2,1,0:T(8,128)S(1)}, f32[16,8,128]{2,1,0:T(8,128)S(1)}, f32[5,16,128]{...) custom-call(s32[2]{0:T(128)S(1)} %pad_add_fusion.place_ref, f32[520,128]{1,0:T(8,128)S(1)} %copy-done.3, ...), custom_call_target="tpu_custom_call" | custom-call | flops 8388608 | bytes 1048576 | tf_op jit(solution)/shard_map/local/pallas_call | solution.py:336
  16.4 0.0 all-to-all-done.got_ref
  16.4 0.0 copy-start.2
  16.4 0.2 middle.1
  16.5 0.0 copy-start
  16.5 0.0 copy-start.1
  16.5 19.6 %all_to_all.10.got_ref = f32[8,32,128]{2,1,0:T(8,128)S(1)} all-to-all(f32[8,32,128]{2,1,0:T(8,128)S(1)} %get-tuple-element.31), channel_id=1, replica_groups={{0,64,128,192,256,320,384,448},{8,72,136,200,264,328,392,456},{16,80,14..., dimensions={0} | all-to-all | bytes 262144 | tf_op jit(solution)/shard_map/all_to_all | solution.py:356
  36.2 0.0 copy-done.2
  36.2 0.0 copy-done
  36.2 0.0 copy-done.1
  36.2 2.5 %final.1 = (bf16[64,1024]{1,0:T(8,128)(2,1)}, bf16[64,1024]{1,0:T(8,128)(2,1)}, bf16[64,1024]{1,0:T(8,128)(2,1)}, f32[16,64]{1,0:T(8,128)}, f32[1,64]{1,0:T(1,128)}) custom-call(f32[8,32,128]{2,1,0:T(8,128)S(1)} %all_to_all.10.got_ref, f32[16,128]{1,0:T(8,128)S(1)} %get-tuple-element.32.enter_ref, f32[5,16,128]{2,1,0:T(8,128)S(1)} %get-tuple-element.29.table_ref, ...), custom_call_target="tpu_custom_call" | custom-call | tf_op jit(solution)/shard_map/final/pallas_call | solution.py:357
  (1 shorter events, 0.0 us)
Async XLA Ops:
  4.0 7.1 %copy-start.3 = (f32[520,128]{1,0:T(8,128)S(1)}, f32[520,128]{1,0:T(8,128)}, u32[]{:S(2)}) copy-start(f32[520,128]{1,0:T(8,128)} %get-tuple-element.25.ut_ref) | copy-start | bytes 798724
  4.0 12.4 %all-to-all-start = ((f32[8,32,128]{2,1,0:T(8,128)}), f32[8,32,128]{2,1,0:T(8,128)S(1)}, u32[]{:S(2)}, u32[]{:S(2)}) async-start(f32[8,32,128]{2,1,0:T(8,128)} %get-tuple-element.24), calls=%async_computation | async-start | bytes 262144 | tf_op jit(solution)/shard_map/all_to_all | solution.py:335
  10.4 0.7 %copy-start.9 = (f32[64,16]{0,1:T(8,128)S(1)}, f32[64,16]{0,1:T(8,128)}, u32[]{:S(2)}) copy-start(f32[64,16]{0,1:T(8,128)} %param.11) | copy-start | bytes 12292
  10.4 0.7 %copy-start.5 = (f32[64,16]{0,1:T(8,128)S(1)}, f32[64,16]{0,1:T(8,128)}, u32[]{:S(2)}) copy-start(f32[64,16]{0,1:T(8,128)} %param.12) | copy-start | bytes 12292
  11.1 0.7 %copy-start.8 = (f32[64]{0:T(128)S(1)}, f32[64]{0:T(128)}, u32[]{:S(2)}) copy-start(f32[64]{0:T(128)} %param.13) | copy-start | bytes 772
  11.7 1.0 %copy-start.4 = (f32[520,128]{1,0:T(8,128)S(1)}, f32[520,128]{1,0:T(8,128)}, u32[]{:S(2)}) copy-start(f32[520,128]{1,0:T(8,128)} %get-tuple-element.26.st_ref) | copy-start | bytes 798724
  12.7 0.8 %copy-start.6 = (f32[16,8,128]{2,1,0:T(8,128)S(1)}, f32[16,8,128]{2,1,0:T(8,128)}, u32[]{:S(2)}) copy-start(f32[16,8,128]{2,1,0:T(8,128)} %get-tuple-element.27.sf_ref) | copy-start | bytes 196612
  13.5 0.8 %copy-start.7 = (f32[16,8,128]{2,1,0:T(8,128)S(1)}, f32[16,8,128]{2,1,0:T(8,128)}, u32[]{:S(2)}) copy-start(f32[16,8,128]{2,1,0:T(8,128)} %get-tuple-element.28.xb_ref) | copy-start | bytes 196612
  16.4 19.8 %copy-start.2 = (bf16[64,1024]{1,0:T(8,128)(2,1)S(1)}, bf16[64,1024]{1,0:T(8,128)(2,1)}, u32[]{:S(2)}) copy-start(bf16[64,1024]{1,0:T(8,128)(2,1)} %g_ref.1) | copy-start | bytes 393220
  16.5 19.6 %copy-start = (bf16[64,1024]{1,0:T(8,128)(2,1)S(1)}, bf16[64,1024]{1,0:T(8,128)(2,1)}, u32[]{:S(2)}) copy-start(bf16[64,1024]{1,0:T(8,128)(2,1)} %k_ref.1) | copy-start | bytes 393220
  16.5 19.6 %copy-start.1 = (bf16[64,1024]{1,0:T(8,128)(2,1)S(1)}, bf16[64,1024]{1,0:T(8,128)(2,1)}, u32[]{:S(2)}) copy-start(bf16[64,1024]{1,0:T(8,128)(2,1)} %v_ref.1) | copy-start | bytes 393220

commit v3 on v2

v3 whole, which is shorter than its diff:
```python
import math

import jax
import jax.numpy as jnp
from jax import lax
from jax.experimental import pallas as pl
from jax.experimental.pallas import tpu as pltpu
from jax.sharding import PartitionSpec as P

MODES = 16
LANES = 128
SUB = 8
HALF = 64
STEPS = 64
PITCH = STEPS + 1
CHUNKS = 16
LOCAL = STEPS * CHUNKS
GROUP = 8
TALL = 16
UNITS = 0
SIGNAL = UNITS + PITCH * SUB
FORWARD = SIGNAL + PITCH * SUB
BACKWARD = FORWARD + MODES * SUB
RATES = BACKWARD + MODES * SUB
GAINS = RATES + MODES
WEIGHTS = GAINS + MODES
SKIPS = WEIGHTS + MODES
PACK = SKIPS + SUB
SUMS = MODES
DIRECT = SUMS + MODES // 2
ROWS = DIRECT + 1
F32 = jnp.float32
NORM = 1.0 / math.sqrt(65536)


def iota(shape, dim):
    return lax.broadcasted_iota(jnp.int32, shape, dim)


def twice(rows):
    return jnp.concatenate([rows, rows], axis=1)


def lift(rows, m):
    return jnp.broadcast_to(rows[m : m + 1], (SUB, LANES))


def to_steps(x, out_ref, base):
    for p in range(4):
        low = x[:, p * LANES : (p + 1) * LANES]
        high = x[:, (p + 4) * LANES : (p + 5) * LANES]
        turned = jnp.concatenate([low, high], axis=0).T
        for q in range(2):
            first = base + (2 * p + q) * PITCH
            out_ref[first : first + STEPS, :] = turned[q * STEPS : (q + 1) * STEPS]


def from_steps(ref, out_ref):
    for p in range(4):
        first = 2 * p * PITCH
        parts = [ref[first : first + STEPS, :], ref[first + PITCH : first + PITCH + STEPS, :]]
        turned = jnp.concatenate(parts, axis=0).T
        out_ref[:, p * LANES : (p + 1) * LANES] = turned[:HALF]
        out_ref[:, (p + 4) * LANES : (p + 5) * LANES] = turned[HALF:]


def turned_rows(rows):
    return jnp.concatenate([rows, jnp.zeros((LANES - MODES, LANES), F32)], axis=0).T


def step_rows(step):
    return pl.ds(step, SUB, stride=PITCH)


def packed_modes(table):
    upper = iota((SUB, LANES), 1) >= HALF
    return jnp.where(upper, table[SUB:], table[:SUB])


def write_message(msg_ref, states, sums, direct):
    for j in range(GROUP):
        first = j * ROWS
        msg_ref[first : first + MODES] = states
        msg_ref[first + SUMS : first + DIRECT] = sums
        msg_ref[first + DIRECT : first + ROWS] = direct


def one_minus_exp(x):
    series = jnp.ones_like(x)
    for n in range(9, 1, -1):
        series = 1.0 - series * (x * (1.0 / n))
    return jnp.where(x < 0.25, x * series, 1.0 - jnp.exp(-x))


def total_of(terms):
    total = terms[0]
    for term in terms[1:]:
        total = total + term
    return total


def added(terms):
    while len(terms) > 1:
        terms = [a + b for a, b in zip(terms[::2], terms[1::2])]
    return terms[0]


def summary_kernel(
    q_any, k_any, v_any, g_any, rate_any, residue_any, skip_any,
    pack_ref, msg_ref,
    q_ref, k_ref, v_ref, g_ref, rate_ref, residue_ref, skip_ref,
    row_ref, decay_ref, sems,
):
    pairs = (
        (rate_any, rate_ref), (k_any, k_ref), (v_any, v_ref), (g_any, g_ref), (q_any, q_ref),
        (residue_any, residue_ref), (skip_any, skip_ref),
    )
    copies = [pltpu.make_async_copy(a, b, sems.at[n]) for n, (a, b) in enumerate(pairs)]
    for copy in copies:
        copy.start()

    copies[0].wait()
    copies[5].wait()
    copies[6].wait()
    rates = twice(rate_ref[...])
    gains = jnp.sqrt(one_minus_exp(2.0 * rates))
    skips = jnp.concatenate([skip_ref[...], skip_ref[...]], axis=1)
    pack_ref[RATES : RATES + MODES] = rates
    pack_ref[GAINS : GAINS + MODES] = gains
    pack_ref[WEIGHTS : WEIGHTS + MODES] = twice(residue_ref[...]) * gains
    pack_ref[SKIPS : SKIPS + SUB] = jnp.broadcast_to(skips, (SUB, LANES))
    row_ref[0] = jnp.exp(-rates)
    row_ref[1] = jnp.exp(-float(STEPS * SUB) * rates)
    for i in range(STEPS // SUB):
        row_ref[2 + i] = jnp.exp(-float(SUB * i) * rates)
    row = iota((SUB, LANES), 0)
    upper = iota((SUB, LANES), 1) >= HALF
    row_f = row.astype(F32)
    chunk = jnp.where(upper, row_f + SUB, row_f)
    for m in range(MODES):
        r = pack_ref[RATES + m : RATES + m + 1, :]
        for n, d in enumerate((1, 2, 4)):
            decay_ref[m, n] = jnp.where(row >= d, jnp.exp(-float(STEPS * d) * r), 0.0)
        decay_ref[m, 3] = jnp.where(upper, jnp.exp(-(STEPS * row_f) * r), 0.0)
        decay_ref[m, 4] = jnp.exp(-(STEPS * chunk) * r)

    copies[1].wait()
    copies[2].wait()
    to_steps(k_ref[...].astype(F32) * v_ref[...].astype(F32), pack_ref, UNITS)
    copies[3].wait()
    copies[4].wait()
    to_steps(g_ref[...].astype(F32) * q_ref[...].astype(F32), pack_ref, SIGNAL)

    zero = jnp.zeros((SUB, LANES), F32)
    ends, adjoints, totals = [], [], []
    lags = [zero] * SUB
    for half in range(2):
        modes = range(half * 8, half * 8 + 8)
        factor = [jnp.exp(-lift(pack_ref, RATES + m)) for m in modes]

        def body(i, carry):
            state, total, back, lags = carry
            u = [pack_ref[step_rows(UNITS + i * SUB + t), :] for t in range(SUB)]
            s = [pack_ref[step_rows(SIGNAL + i * SUB + t), :] for t in range(SUB)]
            part = [s[SUB - 1]] * 8
            for t in reversed(range(SUB - 1)):
                part = [f * p + s[t] for f, p in zip(factor, part)]
            total = [t + x * p for t, x, p in zip(total, state, part)]
            power = [row_ref[2 + i, m : m + 1, :] for m in modes]
            back = [b + w * p for b, w, p in zip(back, power, part)]
            for t in range(SUB):
                state = [f * x + u[t] for f, x in zip(factor, state)]
            if half == 0:
                lags = [
                    lags[d] + total_of([s[t] * u[t - d] for t in range(d, SUB)])
                    for d in range(SUB)
                ]
            return state, total, back, lags

        carry = ([zero] * 8, [zero] * 8, [zero] * 8, lags if half == 0 else [])
        state, total, back, found = lax.fori_loop(0, STEPS // SUB, body, carry, unroll=2)
        if half == 0:
            lags = found
        for n, m in enumerate(modes):
            within = lags[SUB - 1]
            for d in reversed(range(SUB - 1)):
                within = factor[n] * within + lags[d]
            scan = state[n]
            for j, d in enumerate((1, 2, 4)):
                scan = scan + decay_ref[m, j] * pltpu.roll(scan, d, 0)
            last = scan[SUB - 1 : SUB]
            last_other = pltpu.roll(last, HALF, 1)
            start = jnp.where(row >= 1, pltpu.roll(scan, 1, 0), 0.0)
            start = start + decay_ref[m, 3] * last_other
            pack_ref[FORWARD + m * SUB : FORWARD + (m + 1) * SUB] = start
            pack_ref[BACKWARD + m * SUB : BACKWARD + (m + 1) * SUB] = back[n]
            ends.append(last + row_ref[1, m : m + 1, :] * last_other)
            adjoints.append(jnp.sum(decay_ref[m, 4] * back[n], axis=0, keepdims=True))
            cross = factor[n] * (total[n] + start * back[n])
            totals.append(jnp.sum(within + cross, axis=0, keepdims=True))
    ends = jnp.concatenate(ends, axis=0)
    adjoints = jnp.concatenate(adjoints, axis=0)
    totals = jnp.concatenate(totals, axis=0)
    direct = jnp.sum(lags[0], axis=0, keepdims=True)
    adjoints = adjoints + pltpu.roll(adjoints, HALF, 1)
    totals = totals + pltpu.roll(totals, HALF, 1)
    direct = direct + pltpu.roll(direct, HALF, 1)
    lanes_up = iota((MODES, LANES), 1) >= HALF
    write_message(
        msg_ref, jnp.where(lanes_up, ends, adjoints), packed_modes(totals), direct
    )


def local_kernel(
    place_ref, pack_ref,
    mixed_ref, back_ref, after_ref, before_ref, block_ref, table_ref, near_ref, far_ref,
    steps_ref,
):
    rates = pack_ref[RATES : RATES + MODES]
    skip = pack_ref[SKIPS : SKIPS + SUB]
    wide = [lift(rates, m) for m in range(MODES)]
    factor = [jnp.exp(-r) for r in wide]
    weight = [lift(pack_ref, WEIGHTS + m) for m in range(MODES)]

    def run(source, dst_ref, start, flip):
        def body(i, state):
            step = STEPS - 1 - i if flip else i
            x = pack_ref[step_rows(source + step), :]
            state = [f * z + x for f, z in zip(factor, state)]
            dst_ref[step_rows(step), :] = (
                added([w * z for w, z in zip(weight, state)]) + skip * x
            )
            return state

        lax.fori_loop(0, STEPS, body, start, unroll=8)

    row = iota((SUB, LANES), 0)
    upper = iota((SUB, LANES), 1) >= HALF
    run(
        UNITS, steps_ref,
        [pack_ref[FORWARD + m * SUB : FORWARD + (m + 1) * SUB] for m in range(MODES)], False,
    )
    from_steps(steps_ref, mixed_ref)
    start_b = []
    for m in range(MODES):
        scan = pack_ref[BACKWARD + m * SUB : BACKWARD + (m + 1) * SUB]
        for d in (1, 2, 4):
            decay = jnp.where(row < SUB - d, jnp.exp(-float(STEPS * d) * wide[m]), 0.0)
            scan = scan + decay * pltpu.roll(scan, SUB - d, 0)
        first_other = pltpu.roll(lift(scan, 0), HALF, 1)
        start = jnp.where(row < SUB - 1, pltpu.roll(scan, SUB - 1, 0), 0.0)
        decay = jnp.exp(-(STEPS * (SUB - 1 - row).astype(F32)) * wide[m])
        start_b.append(start + jnp.where(upper, 0.0, decay * first_other))
    run(SIGNAL, steps_ref, start_b, True)
    from_steps(steps_ref, back_ref)

    rate_cols = turned_rows(rates)
    weight_cols = turned_rows(pack_ref[WEIGHTS : WEIGHTS + MODES])
    token = iota((HALF, LANES), 1).astype(F32)
    for m in range(MODES):
        r = jnp.broadcast_to(rate_cols[:HALF, m : m + 1], (HALF, LANES))
        w = jnp.broadcast_to(weight_cols[:HALF, m : m + 1], (HALF, LANES))
        after_ref[m] = w * jnp.exp(-(token + 1.0) * r)
        before_ref[m] = w * jnp.exp(-(LANES - token) * r)
        block_ref[m] = jnp.exp(-float(LANES) * r)
    lanes_up = iota((MODES, LANES), 1) >= HALF
    place = place_ref[0]
    ahead = jnp.where(lanes_up, place, GROUP - 1 - place).astype(F32)
    for k in range(GROUP):
        near_ref[k] = jnp.broadcast_to((place == k).astype(F32), (MODES, LANES))
        far_ref[k] = jnp.broadcast_to((place_ref[1] == k).astype(F32), (MODES, LANES))
    table_ref[0] = jnp.exp(-rates)
    table_ref[1] = jnp.exp(-float(LOCAL) * rates)
    table_ref[2] = jnp.exp(-float(LOCAL * GROUP) * rates)
    table_ref[3] = jnp.exp(-(LOCAL * ahead) * rates)
    table_ref[4] = pack_ref[GAINS : GAINS + MODES] * NORM


def combine(got_ref, factor, rho, chosen_ref):
    lanes_up = iota((MODES, LANES), 1) >= HALF
    zero = jnp.zeros((MODES, LANES), F32)
    pairs = [got_ref[k * ROWS : k * ROWS + MODES] for k in range(GROUP)]
    fwd, bwd = zero, zero
    enter_f, enter_b = zero, zero
    cross = zero
    sums = jnp.zeros((SUB, LANES), F32)
    direct = jnp.zeros((1, LANES), F32)
    for k in range(GROUP):
        enter_f = enter_f + chosen_ref[k] * fwd
        cross = cross + fwd * pltpu.roll(pairs[k], HALF, 1)
        fwd = rho * fwd + pairs[k]
        sums = sums + got_ref[k * ROWS + SUMS : k * ROWS + DIRECT]
        direct = direct + got_ref[k * ROWS + DIRECT : (k + 1) * ROWS]
    for k in reversed(range(GROUP)):
        enter_b = enter_b + chosen_ref[k] * bwd
        bwd = rho * bwd + pairs[k]
    entering = jnp.where(lanes_up, enter_f, enter_b)
    joint = jnp.where(lanes_up, fwd, bwd)
    cross = factor * cross
    cross = jnp.where(lanes_up, cross, pltpu.roll(cross, HALF, 1))
    return joint, sums + packed_modes(cross), direct, entering


def middle_kernel(got_ref, table_ref, near_ref, msg_ref, enter_ref):
    joint, sums, direct, entering = combine(got_ref, table_ref[0], table_ref[1], near_ref)
    enter_ref[...] = entering
    write_message(msg_ref, joint, sums, direct)


def final_kernel(
    got_ref, enter_ref, table_ref, far_ref, after_ref, before_ref, block_ref,
    mixed_ref, back_ref, k_ref, v_ref, g_ref,
    gq_any, gk_any, gv_any, gr_any, gs_any,
    gq_ref, gk_ref, gv_ref, gr_ref, gs_ref, enter_cols, full_ref, sems, out_sems,
):
    joint, sums, direct, outer = combine(got_ref, table_ref[0], table_ref[2], far_ref)
    enter_cols[...] = turned_rows(enter_ref[...] + table_ref[3] * outer)
    scaled = sums * packed_modes(table_ref[4])
    gr_ref[0:SUB] = scaled[:, :HALF]
    gr_ref[SUB:MODES] = scaled[:, HALF:]
    gs_ref[...] = direct[:, :HALF] * NORM
    copies = [
        pltpu.make_async_copy(gr_ref, gr_any, sems.at[0]),
        pltpu.make_async_copy(gs_ref, gs_any, sems.at[1]),
    ]
    for copy in copies:
        copy.start()

    def one_way(rows, unit_ref, local_ref, enter, blocks, slot, half):
        parts = [unit_ref[m, rows, :] * enter[:, m : m + 1] for m in range(MODES)]
        for n, b in enumerate(blocks):
            cols = slice(b * LANES, (b + 1) * LANES)
            full_ref[slot, half * SUB : (half + 1) * SUB, cols] = local_ref[rows, cols] + added(
                parts
            )
            if n < len(blocks) - 1:
                parts = [x * block_ref[m, rows, :] for m, x in enumerate(parts)]

    def out_copies(i):
        rows = pl.ds(pl.multiple_of(i * TALL, TALL), TALL)
        pairs = ((gq_ref, gq_any), (gk_ref, gk_any), (gv_ref, gv_any))
        return [
            pltpu.make_async_copy(a.at[rows, :], b.at[rows, :], out_sems.at[n, i])
            for n, (a, b) in enumerate(pairs)
        ]

    def body(i, carry):
        for half in range(2):
            first = pl.multiple_of(i * TALL + half * SUB, SUB)
            rows = pl.ds(first, SUB)
            enter_b = enter_cols[rows, :]
            enter_f = enter_cols[pl.ds(HALF + first, SUB), :]
            one_way(rows, after_ref, mixed_ref, enter_f, range(8), 0, half)
            one_way(rows, before_ref, back_ref, enter_b, range(7, -1, -1), 1, half)
        rows = pl.ds(pl.multiple_of(i * TALL, TALL), TALL)
        for b in range(8):
            cols = slice(b * LANES, (b + 1) * LANES)
            mixed, back = full_ref[0, :, cols], full_ref[1, :, cols]
            gq_ref[rows, cols] = (g_ref[rows, cols].astype(F32) * mixed).astype(jnp.bfloat16)
            gk_ref[rows, cols] = (v_ref[rows, cols].astype(F32) * back).astype(jnp.bfloat16)
            gv_ref[rows, cols] = (k_ref[rows, cols].astype(F32) * back).astype(jnp.bfloat16)
        for copy in out_copies(i):
            copy.start()
        return carry

    lax.fori_loop(0, HALF // TALL, body, 0, unroll=4)
    for i in range(HALF // TALL):
        copies.extend(out_copies(i))
    for copy in copies:
        copy.wait()


VMEM = pl.BlockSpec(memory_space=pltpu.VMEM)
SMEM = pl.BlockSpec(memory_space=pltpu.SMEM)
ANY = pl.BlockSpec(memory_space=pl.ANY)
PARAMS = pltpu.CompilerParams(vmem_limit_bytes=32 * 1024 * 1024)
MESSAGE = jax.ShapeDtypeStruct((GROUP * ROWS, LANES), F32)


def exchange(msg, groups):
    rows = msg.reshape(GROUP * ROWS, 1, LANES)
    rows = lax.all_to_all(rows, "ctx", 0, 0, axis_index_groups=groups, tiled=True)
    return rows.reshape(GROUP * ROWS, LANES)


def shards(queries, keys, values, grad_out, residues, decay_rate, skip_gain):
    me = lax.axis_index("ctx")
    place = jnp.stack([me % GROUP, me // GROUP]).astype(jnp.int32)
    near = [[z * GROUP + k for k in range(GROUP)] for z in range(GROUP)]
    far = [[z * GROUP + k for z in range(GROUP)] for k in range(GROUP)]
    wide = jax.ShapeDtypeStruct(queries.shape, jnp.bfloat16)
    held = pltpu.VMEM(queries.shape, jnp.bfloat16)

    stepped = pltpu.VMEM((PITCH * SUB, LANES), F32)
    small = pltpu.VMEM((MODES, HALF), F32)
    packed = jax.ShapeDtypeStruct((PACK, LANES), F32)
    sources = (
        queries, keys, values, grad_out,
        decay_rate.T, residues.T, skip_gain.reshape(1, HALF),
    )
    pack, msg = pl.pallas_call(
        summary_kernel,
        out_shape=(packed, MESSAGE),
        in_specs=[ANY] * 7,
        out_specs=(VMEM,) * 2,
        scratch_shapes=[held] * 4
        + [small, small, pltpu.VMEM((1, HALF), F32)]
        + [pltpu.VMEM((2 + STEPS // SUB, MODES, LANES), F32)]
        + [pltpu.VMEM((MODES, 5, SUB, LANES), F32), pltpu.SemaphoreType.DMA((7,))],
        compiler_params=PARAMS,
        name="summary",
    )(*(pltpu.with_memory_space_constraint(x, pltpu.HBM) for x in sources))
    got = exchange(msg, near)
    natural = jax.ShapeDtypeStruct(queries.shape, F32)
    units = jax.ShapeDtypeStruct((MODES, HALF, LANES), F32)
    mixed, back, after, before, block, table, near_at, far_at = pl.pallas_call(
        local_kernel,
        out_shape=(natural, natural, units, units, units)
        + tuple(jax.ShapeDtypeStruct((n, MODES, LANES), F32) for n in (5, GROUP, GROUP)),
        in_specs=[SMEM, VMEM],
        out_specs=(VMEM,) * 8,
        scratch_shapes=[stepped],
        compiler_params=PARAMS,
        cost_estimate=pl.CostEstimate(
            flops=8 * STEPS * MODES * SUB * LANES, bytes_accessed=1 << 20, transcendentals=0
        ),
        name="local",
    )(place, pack)
    msg, enter = pl.pallas_call(
        middle_kernel,
        out_shape=(MESSAGE, jax.ShapeDtypeStruct((MODES, LANES), F32)),
        in_specs=[VMEM] * 3,
        out_specs=(VMEM,) * 2,
        compiler_params=PARAMS,
        name="middle",
    )(got, table, near_at)
    got = exchange(msg, far)
    grad_q, grad_k, grad_v, grad_res, grad_skip = pl.pallas_call(
        final_kernel,
        out_shape=(
            wide,
            wide,
            wide,
            jax.ShapeDtypeStruct((MODES, HALF), F32),
            jax.ShapeDtypeStruct((1, HALF), F32),
        ),
        in_specs=[VMEM] * 12,
        out_specs=(ANY,) * 5,
        scratch_shapes=[held] * 3
        + [small, pltpu.VMEM((1, HALF), F32), pltpu.VMEM((LANES, LANES), F32)]
        + [pltpu.VMEM((2, TALL, queries.shape[1]), F32)]
        + [pltpu.SemaphoreType.DMA((2,)), pltpu.SemaphoreType.DMA((3, HALF // TALL))],
        compiler_params=PARAMS,
        name="final",
    )(got, enter, table, far_at, after, before, block, mixed, back, keys, values, grad_out)
    return (grad_q, grad_k, grad_v, grad_res.T, grad_skip.reshape(HALF))


def solution(mesh):
    in_specs = (
        P("tp", "ctx"),
        P("tp", "ctx"),
        P("tp", "ctx"),
        P("tp", "ctx"),
        P("tp", None),
        P("tp", None),
        P("tp"),
    )
    out_specs = (P("tp", "ctx"), P("tp", "ctx"), P("tp", "ctx"), P("tp", None), P("tp"))
    return jax.shard_map(shards, mesh=mesh, in_specs=in_specs, out_specs=out_specs, check_vma=False)
```

time: 39.1 us -> 36.2 us (0.926)
  the two profiles are of different devices: /device:TPU:56 before, /device:TPU:6 now
where the time goes in v3:
time: 36.2 us; the launch traced here: 35.9 us
  blocking collectives  19 us (52%)
  Pallas kernels  7.41 us (20%)
  starting transfers between devices  4.89 us (14%)
  waiting for transfers between devices  3.88 us (11%)
  between operations  0.65 us (2%)
    all_to_all x1, blocking collectives, exchange(): lax.all_to_all(rows, 'ctx', 0, 0, axis_index_groups=groups, tiled=True)  19 us
    all_to_all x1, starting transfers between devices, exchange(): lax.all_to_all(rows, 'ctx', 0, 0, axis_index_groups=groups, tiled=True)  4.89 us
    all_to_all x1, waiting for transfers between devices, exchange(): lax.all_to_all(rows, 'ctx', 0, 0, axis_index_groups=groups, tiled=True)  3.88 us
    pallas_call x1, Pallas kernels, shards(): pl.pallas_call(summary_kernel, out_shape=(packed, MESSAGE), in_specs=[ANY...  3.11 us
    pallas_call x1, Pallas kernels, shards(): pl.pallas_call(local_kernel, out_shape=(natural, natural, units, units, u...  2.44 us
    pallas_call x1, Pallas kernels, shards(): pl.pallas_call(final_kernel, out_shape=(wide, wide, wide, jax.ShapeDtypeS...  1.7 us
  transfers between devices with their start and end apart: 1, of which 1 were waited for; matrix products, arithmetic and copies ran while one was open for 0% of the time, Pallas kernels for 7%

profile of v3, /device:TPU:6, one launch (start us, length us, event | category | flops | bytes accessed | tf_op | source)
XLA Modules:
  0.0 35.9 jit_solution(16480746001689779433)
XLA Ops:
  0.6 3.1 %summary.1 = (f32[1352,128]{1,0:T(8,128)S(1)}, f32[200,128]{1,0:T(8,128)}) custom-call(bf16[64,1024]{1,0:T(8,128)(2,1)} %q_any.1, bf16[64,1024]{1,0:T(8,128)(2,1)} %k_ref.1, bf16[64,1024]{1,0:T(8,128)(2,1)} %v_ref.1, bf16[64,1024]{1,0:T(8,128)(2,1)} %g_ref.1, f32[16,64]{1,0:T(8,128)} %bitcast.18, f32[16,64]{1,0:T(8,128)} %bitcast.19, f32[1,64]{1,0:T(1,128)} %bitcast.20), custom_call_target="tpu_custom_call" | custom-call | tf_op jit(solution)/shard_map/summary/pallas_call | solution.py:401
  3.7 4.9 %all-to-all-start = ((f32[200,1,128]{2,1,0:T(1,128)}), f32[200,1,128]{2,1,0:T(1,128)S(1)}, u32[]{:S(2)}, u32[]{:S(2)}) async-start(f32[200,1,128]{2,1,0:T(1,128)} %bitcast.4), calls=%async_computation | async-start | bytes 204800 | tf_op jit(solution)/shard_map/all_to_all | solution.py:382
  8.6 0.1 pad_add_fusion.place_ref
  8.7 2.4 %local.1 = (f32[64,1024]{1,0:T(8,128)S(1)}, f32[64,1024]{1,0:T(8,128)S(1)}, f32[16,64,128]{2,1,0:T(8,128)S(1)}, f32[16,64,128]{2,1,0:T(8,128)S(1)}, f32[16,64,12...) custom-call(s32[2]{0:T(128)S(1)} %pad_add_fusion.place_ref, ...), custom_call_target="tpu_custom_call" | custom-call | flops 8388608 | bytes 1048576 | tf_op jit(solution)/shard_map/local/pallas_call | solution.py:416
  11.2 3.9 %all-to-all-done = f32[200,1,128]{2,1,0:T(1,128)S(1)} async-done(((f32[200,1,128]{2,1,0:T(1,128)}), f32[200,1,128]{2,1,0:T(1,128)S(1)}, u32[]{:S(2)}, u32[]{:S(2)}) %all-to-all-start) | async-done | bytes 102432 | tf_op jit(solution)/shard_map/all_to_all | solution.py:382
  15.0 0.0 copy-start.1
  15.0 0.0 copy-start.2
  15.0 0.2 middle.1
  15.2 0.0 copy-start
  15.2 19.0 %all_to_all.10 = f32[200,1,128]{2,1,0:T(1,128)S(1)} all-to-all(f32[200,1,128]{2,1,0:T(1,128)S(1)} %bitcast.17), channel_id=1, replica_groups={{0,64,128,192,256,320,384,448},{8,72,136,200,264,328,392,456},{16,80,14..., dimensions={0} | all-to-all | bytes 204800 | tf_op jit(solution)/shard_map/all_to_all | solution.py:382
  34.2 0.0 copy-done.1
  34.2 0.0 copy-done.2
  34.2 0.0 copy-done
  34.2 1.7 %final.1 = (bf16[64,1024]{1,0:T(8,128)(2,1)}, bf16[64,1024]{1,0:T(8,128)(2,1)}, bf16[64,1024]{1,0:T(8,128)(2,1)}, f32[16,64]{1,0:T(8,128)}, f32[1,64]{1,0:T(1,128)}) custom-call(f32[200,128]{1,0:T(8,128)S(1)} %bitcast.16, f32[16,128]{1,0:T(8,128)S(1)} %get-tuple-element.27.enter_ref, f32[5,16,128]{2,1,0:T(8,128)S(1)} %get-tuple-element.24.table_ref, ...), custom_call_target="tpu_custom_call" | custom-call | tf_op jit(solution)/shard_map/final/pallas_call | solution.py:438
Async XLA Ops:
  3.7 11.3 %all-to-all-start = ((f32[200,1,128]{2,1,0:T(1,128)}), f32[200,1,128]{2,1,0:T(1,128)S(1)}, u32[]{:S(2)}, u32[]{:S(2)}) async-start(f32[200,1,128]{2,1,0:T(1,128)} %bitcast.4), calls=%async_computation | async-start | bytes 204800 | tf_op jit(solution)/shard_map/all_to_all | solution.py:382
  15.0 19.2 %copy-start.1 = (bf16[64,1024]{1,0:T(8,128)(2,1)S(1)}, bf16[64,1024]{1,0:T(8,128)(2,1)}, u32[]{:S(2)}) copy-start(bf16[64,1024]{1,0:T(8,128)(2,1)} %v_ref.1) | copy-start | bytes 393220
  15.0 19.2 %copy-start.2 = (bf16[64,1024]{1,0:T(8,128)(2,1)S(1)}, bf16[64,1024]{1,0:T(8,128)(2,1)}, u32[]{:S(2)}) copy-start(bf16[64,1024]{1,0:T(8,128)(2,1)} %g_ref.1) | copy-start | bytes 393220
  15.2 19.0 %copy-start = (bf16[64,1024]{1,0:T(8,128)(2,1)S(1)}, bf16[64,1024]{1,0:T(8,128)(2,1)}, u32[]{:S(2)}) copy-start(bf16[64,1024]{1,0:T(8,128)(2,1)} %k_ref.1) | copy-start | bytes 393220

commit v4 on v3

--- a/solution.py
+++ b/solution.py
@@ -16,6 +16,8 @@
 CHUNKS = 16
 LOCAL = STEPS * CHUNKS
 GROUP = 8
+NEAR_ORDER = tuple((k + 5) % GROUP for k in range(GROUP))
+FAR_ORDER = tuple((k + 5) % GROUP for k in range(GROUP))
 TALL = 16
 UNITS = 0
 SIGNAL = UNITS + PITCH * SUB
@@ -107,7 +109,7 @@
 
 def summary_kernel(
     q_any, k_any, v_any, g_any, rate_any, residue_any, skip_any,
-    pack_ref, msg_ref,
+    pack_ref, msg_ref, near_ref,
     q_ref, k_ref, v_ref, g_ref, rate_ref, residue_ref, skip_ref,
     row_ref, decay_ref, sems,
 ):
@@ -130,6 +132,8 @@
     pack_ref[WEIGHTS : WEIGHTS + MODES] = twice(residue_ref[...]) * gains
     pack_ref[SKIPS : SKIPS + SUB] = jnp.broadcast_to(skips, (SUB, LANES))
     row_ref[0] = jnp.exp(-rates)
+    near_ref[0] = jnp.exp(-rates)
+    near_ref[1] = jnp.exp(-float(LOCAL) * rates)
     row_ref[1] = jnp.exp(-float(STEPS * SUB) * rates)
     for i in range(STEPS // SUB):
         row_ref[2 + i] = jnp.exp(-float(SUB * i) * rates)
@@ -212,8 +216,8 @@
 
 
 def local_kernel(
-    place_ref, pack_ref,
-    mixed_ref, back_ref, after_ref, before_ref, block_ref, table_ref, near_ref, far_ref,
+    pack_ref,
+    mixed_ref, back_ref, after_ref, before_ref, block_ref, table_ref,
     steps_ref,
 ):
     rates = pack_ref[RATES : RATES + MODES]
@@ -264,35 +268,32 @@
         before_ref[m] = w * jnp.exp(-(LANES - token) * r)
         block_ref[m] = jnp.exp(-float(LANES) * r)
     lanes_up = iota((MODES, LANES), 1) >= HALF
-    place = place_ref[0]
+    place = lax.rem(lax.axis_index("ctx"), GROUP)
     ahead = jnp.where(lanes_up, place, GROUP - 1 - place).astype(F32)
-    for k in range(GROUP):
-        near_ref[k] = jnp.broadcast_to((place == k).astype(F32), (MODES, LANES))
-        far_ref[k] = jnp.broadcast_to((place_ref[1] == k).astype(F32), (MODES, LANES))
     table_ref[0] = jnp.exp(-rates)
-    table_ref[1] = jnp.exp(-float(LOCAL) * rates)
-    table_ref[2] = jnp.exp(-float(LOCAL * GROUP) * rates)
-    table_ref[3] = jnp.exp(-(LOCAL * ahead) * rates)
-    table_ref[4] = pack_ref[GAINS : GAINS + MODES] * NORM
-
-
-def combine(got_ref, factor, rho, chosen_ref):
+    table_ref[1] = jnp.exp(-float(LOCAL * GROUP) * rates)
+    table_ref[2] = jnp.exp(-(LOCAL * ahead) * rates)
+    table_ref[3] = pack_ref[GAINS : GAINS + MODES] * NORM
+
+
+def combine(got_ref, order, factor, rho, place):
     lanes_up = iota((MODES, LANES), 1) >= HALF
     zero = jnp.zeros((MODES, LANES), F32)
-    pairs = [got_ref[k * ROWS : k * ROWS + MODES] for k in range(GROUP)]
+    firsts = [order.index(k) * ROWS for k in range(GROUP)]
+    pairs = [got_ref[f : f + MODES] for f in firsts]
     fwd, bwd = zero, zero
     enter_f, enter_b = zero, zero
     cross = zero
     sums = jnp.zeros((SUB, LANES), F32)
     direct = jnp.zeros((1, LANES), F32)
     for k in range(GROUP):
-        enter_f = enter_f + chosen_ref[k] * fwd
+        enter_f = jnp.where(place == k, fwd, enter_f)
         cross = cross + fwd * pltpu.roll(pairs[k], HALF, 1)
         fwd = rho * fwd + pairs[k]
-        sums = sums + got_ref[k * ROWS + SUMS : k * ROWS + DIRECT]
-        direct = direct + got_ref[k * ROWS + DIRECT : (k + 1) * ROWS]
+        sums = sums + got_ref[firsts[k] + SUMS : firsts[k] + DIRECT]
+        direct = direct + got_ref[firsts[k] + DIRECT : firsts[k] + ROWS]
     for k in reversed(range(GROUP)):
-        enter_b = enter_b + chosen_ref[k] * bwd
+        enter_b = jnp.where(place == k, bwd, enter_b)
         bwd = rho * bwd + pairs[k]
     entering = jnp.where(lanes_up, enter_f, enter_b)
     joint = jnp.where(lanes_up, fwd, bwd)
@@ -301,21 +302,25 @@
     return joint, sums + packed_modes(cross), direct, entering
 
 
-def middle_kernel(got_ref, table_ref, near_ref, msg_ref, enter_ref):
-    joint, sums, direct, entering = combine(got_ref, table_ref[0], table_ref[1], near_ref)
+def middle_kernel(got_ref, near_ref, msg_ref, enter_ref):
+    joint, sums, direct, entering = combine(
+        got_ref, NEAR_ORDER, near_ref[0], near_ref[1], lax.rem(lax.axis_index("ctx"), GROUP)
+    )
     enter_ref[...] = entering
     write_message(msg_ref, joint, sums, direct)
 
 
 def final_kernel(
-    got_ref, enter_ref, table_ref, far_ref, after_ref, before_ref, block_ref,
+    got_ref, enter_ref, table_ref, after_ref, before_ref, block_ref,
     mixed_ref, back_ref, k_ref, v_ref, g_ref,
     gq_any, gk_any, gv_any, gr_any, gs_any,
     gq_ref, gk_ref, gv_ref, gr_ref, gs_ref, enter_cols, full_ref, sems, out_sems,
 ):
-    joint, sums, direct, outer = combine(got_ref, table_ref[0], table_ref[2], far_ref)
-    enter_cols[...] = turned_rows(enter_ref[...] + table_ref[3] * outer)
-    scaled = sums * packed_modes(table_ref[4])
+    joint, sums, direct, outer = combine(
+        got_ref, FAR_ORDER, table_ref[0], table_ref[1], lax.div(lax.axis_index("ctx"), GROUP)
+    )
+    enter_cols[...] = turned_rows(enter_ref[...] + table_ref[2] * outer)
+    scaled = sums * packed_modes(table_ref[3])
     gr_ref[0:SUB] = scaled[:, :HALF]
     gr_ref[SUB:MODES] = scaled[:, HALF:]
     gs_ref[...] = direct[:, :HALF] * NORM
@@ -371,7 +376,6 @@
 
 
 VMEM = pl.BlockSpec(memory_space=pltpu.VMEM)
-SMEM = pl.BlockSpec(memory_space=pltpu.SMEM)
 ANY = pl.BlockSpec(memory_space=pl.ANY)
 PARAMS = pltpu.CompilerParams(vmem_limit_bytes=32 * 1024 * 1024)
 MESSAGE = jax.ShapeDtypeStruct((GROUP * ROWS, LANES), F32)
@@ -384,10 +388,8 @@
 
 
 def shards(queries, keys, values, grad_out, residues, decay_rate, skip_gain):
-    me = lax.axis_index("ctx")
-    place = jnp.stack([me % GROUP, me // GROUP]).astype(jnp.int32)
-    near = [[z * GROUP + k for k in range(GROUP)] for z in range(GROUP)]
-    far = [[z * GROUP + k for z in range(GROUP)] for k in range(GROUP)]
+    near = [[z * GROUP + k for k in NEAR_ORDER] for z in range(GROUP)]
+    far = [[z * GROUP + k for z in FAR_ORDER] for k in range(GROUP)]
     wide = jax.ShapeDtypeStruct(queries.shape, jnp.bfloat16)
     held = pltpu.VMEM(queries.shape, jnp.bfloat16)
 
@@ -398,11 +400,11 @@
         queries, keys, values, grad_out,
         decay_rate.T, residues.T, skip_gain.reshape(1, HALF),
     )
-    pack, msg = pl.pallas_call(
+    pack, msg, near_table = pl.pallas_call(
         summary_kernel,
-        out_shape=(packed, MESSAGE),
+        out_shape=(packed, MESSAGE, jax.ShapeDtypeStruct((2, MODES, LANES), F32)),
         in_specs=[ANY] * 7,
-        out_specs=(VMEM,) * 2,
+        out_specs=(VMEM,) * 3,
         scratch_shapes=[held] * 4
         + [small, small, pltpu.VMEM((1, HALF), F32)]
         + [pltpu.VMEM((2 + STEPS // SUB, MODES, LANES), F32)]
@@ -411,29 +413,30 @@
         name="summary",
     )(*(pltpu.with_memory_space_constraint(x, pltpu.HBM) for x in sources))
     got = exchange(msg, near)
+    msg, enter = pl.pallas_call(
+        middle_kernel,
+        out_shape=(MESSAGE, jax.ShapeDtypeStruct((MODES, LANES), F32)),
+        in_specs=[VMEM] * 2,
+        out_specs=(VMEM,) * 2,
+        compiler_params=PARAMS,
+        name="middle",
+    )(got, near_table)
+    pack, enter = lax.optimization_barrier((pack, enter))
     natural = jax.ShapeDtypeStruct(queries.shape, F32)
     units = jax.ShapeDtypeStruct((MODES, HALF, LANES), F32)
-    mixed, back, after, before, block, table, near_at, far_at = pl.pallas_call(
+    mixed, back, after, before, block, table = pl.pallas_call(
         local_kernel,
         out_shape=(natural, natural, units, units, units)
-        + tuple(jax.ShapeDtypeStruct((n, MODES, LANES), F32) for n in (5, GROUP, GROUP)),
-        in_specs=[SMEM, VMEM],
-        out_specs=(VMEM,) * 8,
+        + (jax.ShapeDtypeStruct((4, MODES, LANES), F32),),
+        in_specs=[VMEM],
+        out_specs=(VMEM,) * 6,
         scratch_shapes=[stepped],
         compiler_params=PARAMS,
         cost_estimate=pl.CostEstimate(
             flops=8 * STEPS * MODES * SUB * LANES, bytes_accessed=1 << 20, transcendentals=0
         ),
         name="local",
-    )(place, pack)
-    msg, enter = pl.pallas_call(
-        middle_kernel,
-        out_shape=(MESSAGE, jax.ShapeDtypeStruct((MODES, LANES), F32)),
-        in_specs=[VMEM] * 3,
-        out_specs=(VMEM,) * 2,
-        compiler_params=PARAMS,
-        name="middle",
-    )(got, table, near_at)
+    )(pack)
     got = exchange(msg, far)
     grad_q, grad_k, grad_v, grad_res, grad_skip = pl.pallas_call(
         final_kernel,
@@ -444,7 +447,7 @@
             jax.ShapeDtypeStruct((MODES, HALF), F32),
             jax.ShapeDtypeStruct((1, HALF), F32),
         ),
-        in_specs=[VMEM] * 12,
+        in_specs=[VMEM] * 11,
         out_specs=(ANY,) * 5,
         scratch_shapes=[held] * 3
         + [small, pltpu.VMEM((1, HALF), F32), pltpu.VMEM((LANES, LANES), F32)]
@@ -452,7 +455,7 @@
         + [pltpu.SemaphoreType.DMA((2,)), pltpu.SemaphoreType.DMA((3, HALF // TALL))],
         compiler_params=PARAMS,
         name="final",
-    )(got, enter, table, far_at, after, before, block, mixed, back, keys, values, grad_out)
+    )(got, enter, table, after, before, block, mixed, back, keys, values, grad_out)
     return (grad_q, grad_k, grad_v, grad_res.T, grad_skip.reshape(HALF))
 
 

time: 36.2 us -> 31.7 us (0.88)
  blocking collectives: 19 us -> 8.99 us
  starting transfers between devices: 4.89 us -> 12.7 us
  waiting for transfers between devices: 3.88 us -> 2.22 us
  Pallas kernels: 7.41 us -> 6.87 us
    all_to_all x1, blocking collectives: 19 us -> 8.99 us  [exchange(): lax.all_to_all(rows, 'ctx', 0, 0, axis_index_groups=groups, tiled=True)]
    all_to_all x1, starting transfers between devices: 4.89 us -> 12.7 us  [exchange(): lax.all_to_all(rows, 'ctx', 0, 0, axis_index_groups=groups, tiled=True)]
    all_to_all x1, waiting for transfers between devices: 3.88 us -> 2.22 us  [exchange(): lax.all_to_all(rows, 'ctx', 0, 0, axis_index_groups=groups, tiled=True)]
    pallas_call x1, Pallas kernels: 3.11 us -> 2.47 us  [shards(): pl.pallas_call(summary_kernel, out_shape=(packed, MESSAGE, jax.ShapeDtype...]
    pallas_call x1, Pallas kernels: 0.16 us -> 0.8 us  [shards(): pl.pallas_call(middle_kernel, out_shape=(MESSAGE, jax.ShapeDtypeStruct((M...]
    pallas_call x1, Pallas kernels: 2.44 us -> 1.9 us  [shards(): pl.pallas_call(local_kernel, out_shape=(natural, natural, units, units, u...]
  transfers between devices with their start and end apart: 1 -> 1, of which waited for: 1 -> 1; matrix products, arithmetic and copies ran while one was open for 0% -> 0% of each run, Pallas kernels for 7% -> 6%
where the time goes in v4:
time: 31.7 us; the launch traced here: 31.4 us
  starting transfers between devices  12.7 us (40%)
  blocking collectives  8.99 us (28%)
  Pallas kernels  6.87 us (22%)
  waiting for transfers between devices  2.22 us (7%)
  between operations  0.66 us (2%)
    all_to_all x1, starting transfers between devices, exchange(): lax.all_to_all(rows, 'ctx', 0, 0, axis_index_groups=groups, tiled=True)  12.7 us
    all_to_all x1, blocking collectives, exchange(): lax.all_to_all(rows, 'ctx', 0, 0, axis_index_groups=groups, tiled=True)  8.99 us
    pallas_call x1, Pallas kernels, shards(): pl.pallas_call(summary_kernel, out_shape=(packed, MESSAGE, jax.ShapeDtype...  2.47 us
    all_to_all x1, waiting for transfers between devices, exchange(): lax.all_to_all(rows, 'ctx', 0, 0, axis_index_groups=groups, tiled=True)  2.22 us
    pallas_call x1, Pallas kernels, shards(): pl.pallas_call(local_kernel, out_shape=(natural, natural, units, units, u...  1.9 us
    pallas_call x1, Pallas kernels, shards(): pl.pallas_call(final_kernel, out_shape=(wide, wide, wide, jax.ShapeDtypeS...  1.69 us
    pallas_call x1, Pallas kernels, shards(): pl.pallas_call(middle_kernel, out_shape=(MESSAGE, jax.ShapeDtypeStruct((M...  0.8 us
  transfers between devices with their start and end apart: 1, of which 1 were waited for; matrix products, arithmetic and copies ran while one was open for 0% of the time, Pallas kernels for 6%

profile of v4, /device:TPU:6, one launch (start us, length us, event | category | flops | bytes accessed | tf_op | source)
XLA Modules:
  0.0 31.4 jit_solution(2295230608889622666)
XLA Ops:
  0.6 2.5 %summary.1 = (f32[1352,128]{1,0:T(8,128)S(1)}, f32[200,128]{1,0:T(8,128)S(1)}, f32[2,16,128]{2,1,0:T(8,128)S(1)}) custom-call(bf16[64,1024]{1,0:T(8,128)(2,1)} %q_any.1, bf16[64,1024]{1,0:T(8,128)(2,1)} %k_ref.1, bf16[64,1024]{1,0:T(8,128)(2,1)} %v_ref.1, bf16[64,1024]{1,0:T(8,128)(2,1)} %g_ref.1, f32[16,64]{1,0:T(8,128)} %bitcast.16, f32[16,64]{1,0:T(8,128)} %bitcast.17, ...), custom_call_target="tpu_custom_call" | custom-call | tf_op jit(solution)/shard_map/summary/pallas_call | solution.py:403
  3.1 9.0 %all_to_all.10 = f32[200,1,128]{2,1,0:T(1,128)S(1)} all-to-all(f32[200,1,128]{2,1,0:T(1,128)S(1)} %bitcast.15), channel_id=1, replica_groups={{40,48,56,0,8,16,24,32},{104,112,120,64,72,80,88,96},{168,176,184,128,1..., dimensions={0} | all-to-all | bytes 204800 | tf_op jit(solution)/shard_map/all_to_all | solution.py:386
  12.1 0.8 %middle.1 = (f32[200,128]{1,0:T(8,128)}, f32[16,128]{1,0:T(8,128)S(1)}) custom-call(f32[200,128]{1,0:T(8,128)S(1)} %bitcast.13, f32[2,16,128]{2,1,0:T(8,128)S(1)} %get-tuple-element.24.near_ref), custom_call_target="tpu_custom_call" | custom-call | tf_op jit(solution)/shard_map/middle/pallas_call | solution.py:416
  12.9 12.7 %all-to-all-start.1 = ((f32[200,1,128]{2,1,0:T(1,128)}), f32[200,1,128]{2,1,0:T(1,128)S(1)}, u32[]{:S(2)}, u32[]{:S(2)}) async-start(f32[200,1,128]{2,1,0:T(1,128)} %bitcast.7), calls=%async_computation.1 | async-start | bytes 204800 | tf_op jit(solution)/shard_map/all_to_all | solution.py:386
  25.6 0.0 copy-start
  25.6 0.0 copy-start.1
  25.6 0.0 copy-start.2
  25.6 1.9 %local.1 = (f32[64,1024]{1,0:T(8,128)S(1)}, f32[64,1024]{1,0:T(8,128)S(1)}, f32[16,64,128]{2,1,0:T(8,128)S(1)}, f32[16,64,128]{2,1,0:T(8,128)S(1)}, f32[16,64,12...) custom-call(f32[1352,128]{1,0:T(8,128)S(1)} %get-tuple-element.29.pack_ref), custom_call_target="tpu_custom_call" | custom-call | flops 8388608 | bytes 1048576 | tf_op jit(solution)/shard_map/local/pallas_call | solution.py:427
  27.5 2.2 %all-to-all-done.1 = f32[200,1,128]{2,1,0:T(1,128)S(1)} async-done(((f32[200,1,128]{2,1,0:T(1,128)}), f32[200,1,128]{2,1,0:T(1,128)S(1)}, u32[]{:S(2)}, u32[]{:S(2)}) %all-to-all-start.1) | async-done | bytes 102432 | tf_op jit(solution)/shard_map/all_to_all | solution.py:386
  29.7 0.0 copy-done
  29.7 0.0 copy-done.1
  29.7 0.0 copy-done.2
  29.7 1.7 %final.1 = (bf16[64,1024]{1,0:T(8,128)(2,1)}, bf16[64,1024]{1,0:T(8,128)(2,1)}, bf16[64,1024]{1,0:T(8,128)(2,1)}, f32[16,64]{1,0:T(8,128)}, f32[1,64]{1,0:T(1,128)}) custom-call(f32[200,128]{1,0:T(8,128)S(1)} %bitcast.14, f32[16,128]{1,0:T(8,128)S(1)} %get-tuple-element.28.enter_ref, f32[4,16,128]{2,1,0:T(8,128)S(1)} %get-tuple-element.30.table_ref, ...), custom_call_target="tpu_custom_call" | custom-call | tf_op jit(solution)/shard_map/final/pallas_call | solution.py:441
Async XLA Ops:
  12.9 16.8 %all-to-all-start.1 = ((f32[200,1,128]{2,1,0:T(1,128)}), f32[200,1,128]{2,1,0:T(1,128)S(1)}, u32[]{:S(2)}, u32[]{:S(2)}) async-start(f32[200,1,128]{2,1,0:T(1,128)} %bitcast.7), calls=%async_computation.1 | async-start | bytes 204800 | tf_op jit(solution)/shard_map/all_to_all | solution.py:386
  25.6 4.1 %copy-start = (bf16[64,1024]{1,0:T(8,128)(2,1)S(1)}, bf16[64,1024]{1,0:T(8,128)(2,1)}, u32[]{:S(2)}) copy-start(bf16[64,1024]{1,0:T(8,128)(2,1)} %k_ref.1) | copy-start | bytes 393220
  25.6 4.1 %copy-start.1 = (bf16[64,1024]{1,0:T(8,128)(2,1)S(1)}, bf16[64,1024]{1,0:T(8,128)(2,1)}, u32[]{:S(2)}) copy-start(bf16[64,1024]{1,0:T(8,128)(2,1)} %v_ref.1) | copy-start | bytes 393220
  25.6 4.1 %copy-start.2 = (bf16[64,1024]{1,0:T(8,128)(2,1)S(1)}, bf16[64,1024]{1,0:T(8,128)(2,1)}, u32[]{:S(2)}) copy-start(bf16[64,1024]{1,0:T(8,128)(2,1)} %g_ref.1) | copy-start | bytes 393220

commit v5 on v4

--- a/solution.py
+++ b/solution.py
@@ -16,6 +16,7 @@
 CHUNKS = 16
 LOCAL = STEPS * CHUNKS
 GROUP = 8
+EARLY = 4
 NEAR_ORDER = tuple((k + 5) % GROUP for k in range(GROUP))
 FAR_ORDER = tuple((k + 5) % GROUP for k in range(GROUP))
 TALL = 16
@@ -215,7 +216,7 @@
     )
 
 
-def local_kernel(
+def local_outputs(
     pack_ref,
     mixed_ref, back_ref, after_ref, before_ref, block_ref, table_ref,
     steps_ref,
@@ -302,17 +303,41 @@
     return joint, sums + packed_modes(cross), direct, entering
 
 
-def middle_kernel(got_ref, near_ref, msg_ref, enter_ref):
+def starts_early():
+    return lax.div(lax.axis_index("ctx"), GROUP) < EARLY
+
+
+def middle_kernel(
+    got_ref, near_ref, pack_ref, msg_ref, enter_ref, *refs
+):
     joint, sums, direct, entering = combine(
         got_ref, NEAR_ORDER, near_ref[0], near_ref[1], lax.rem(lax.axis_index("ctx"), GROUP)
     )
     enter_ref[...] = entering
     write_message(msg_ref, joint, sums, direct)
 
-
-def final_kernel(
-    got_ref, enter_ref, table_ref, after_ref, before_ref, block_ref,
-    mixed_ref, back_ref, k_ref, v_ref, g_ref,
+    @pl.when(starts_early())
+    def _():
+        local_outputs(pack_ref, *refs)
+
+
+def final_kernel(*refs):
+    got, enter, pack, *early = refs[:9]
+    rest, late, steps = refs[9:-7], refs[-7:-1], refs[-1]
+
+    @pl.when(starts_early())
+    def _():
+        finish(got, enter, *early, *rest)
+
+    @pl.when(jnp.logical_not(starts_early()))
+    def _():
+        local_outputs(pack, *late, steps)
+        finish(got, enter, *late, *rest)
+
+
+def finish(
+    got_ref, enter_ref, mixed_ref, back_ref, after_ref, before_ref, block_ref, table_ref,
+    k_ref, v_ref, g_ref,
     gq_any, gk_any, gv_any, gr_any, gs_any,
     gq_ref, gk_ref, gv_ref, gr_ref, gs_ref, enter_cols, full_ref, sems, out_sems,
 ):
@@ -413,30 +438,19 @@
         name="summary",
     )(*(pltpu.with_memory_space_constraint(x, pltpu.HBM) for x in sources))
     got = exchange(msg, near)
-    msg, enter = pl.pallas_call(
+    natural = jax.ShapeDtypeStruct(queries.shape, F32)
+    units = jax.ShapeDtypeStruct((MODES, HALF, LANES), F32)
+    local = (natural, natural, units, units, units)
+    local = local + (jax.ShapeDtypeStruct((4, MODES, LANES), F32),)
+    msg, enter, *early = pl.pallas_call(
         middle_kernel,
-        out_shape=(MESSAGE, jax.ShapeDtypeStruct((MODES, LANES), F32)),
-        in_specs=[VMEM] * 2,
-        out_specs=(VMEM,) * 2,
+        out_shape=(MESSAGE, jax.ShapeDtypeStruct((MODES, LANES), F32)) + local,
+        in_specs=[VMEM] * 3,
+        out_specs=(VMEM,) * 8,
+        scratch_shapes=[stepped],
         compiler_params=PARAMS,
         name="middle",
-    )(got, near_table)
-    pack, enter = lax.optimization_barrier((pack, enter))
-    natural = jax.ShapeDtypeStruct(queries.shape, F32)
-    units = jax.ShapeDtypeStruct((MODES, HALF, LANES), F32)
-    mixed, back, after, before, block, table = pl.pallas_call(
-        local_kernel,
-        out_shape=(natural, natural, units, units, units)
-        + (jax.ShapeDtypeStruct((4, MODES, LANES), F32),),
-        in_specs=[VMEM],
-        out_specs=(VMEM,) * 6,
-        scratch_shapes=[stepped],
-        compiler_params=PARAMS,
-        cost_estimate=pl.CostEstimate(
-            flops=8 * STEPS * MODES * SUB * LANES, bytes_accessed=1 << 20, transcendentals=0
-        ),
-        name="local",
-    )(pack)
+    )(got, near_table, pack)
     got = exchange(msg, far)
     grad_q, grad_k, grad_v, grad_res, grad_skip = pl.pallas_call(
         final_kernel,
@@ -447,15 +461,17 @@
             jax.ShapeDtypeStruct((MODES, HALF), F32),
             jax.ShapeDtypeStruct((1, HALF), F32),
         ),
-        in_specs=[VMEM] * 11,
+        in_specs=[VMEM] * 12,
         out_specs=(ANY,) * 5,
         scratch_shapes=[held] * 3
         + [small, pltpu.VMEM((1, HALF), F32), pltpu.VMEM((LANES, LANES), F32)]
         + [pltpu.VMEM((2, TALL, queries.shape[1]), F32)]
-        + [pltpu.SemaphoreType.DMA((2,)), pltpu.SemaphoreType.DMA((3, HALF // TALL))],
+        + [pltpu.SemaphoreType.DMA((2,)), pltpu.SemaphoreType.DMA((3, HALF // TALL))]
+        + [pltpu.VMEM(x.shape, F32) for x in local]
+        + [stepped],
         compiler_params=PARAMS,
         name="final",
-    )(got, enter, table, after, before, block, mixed, back, keys, values, grad_out)
+    )(got, enter, pack, *early, keys, values, grad_out)
     return (grad_q, grad_k, grad_v, grad_res.T, grad_skip.reshape(HALF))
 
 

time: 31.7 us -> 30.9 us (0.975)
  blocking collectives: 8.99 us -> 23.8 us
  starting transfers between devices: 12.7 us -> 0 us
  waiting for transfers between devices: 2.22 us -> 0 us
  Pallas kernels: 6.87 us -> 6.22 us
    all_to_all x1 -> x2, blocking collectives: 8.99 us -> 23.8 us  [exchange(): lax.all_to_all(rows, 'ctx', 0, 0, axis_index_groups=groups, tiled=True)]
    all_to_all x1 -> x0, starting transfers between devices: 12.7 us -> none  [exchange(): lax.all_to_all(rows, 'ctx', 0, 0, axis_index_groups=groups, tiled=True)]
    all_to_all x1 -> x0, waiting for transfers between devices: 2.22 us -> none  [exchange(): lax.all_to_all(rows, 'ctx', 0, 0, axis_index_groups=groups, tiled=True)]
    pallas_call x1 -> x0, Pallas kernels: 1.9 us -> none  [shards(): pl.pallas_call(local_kernel, out_shape=(natural, natural, units, units, u...]
    pallas_call x1, Pallas kernels: 0.8 us -> 2.06 us  [shards(): pl.pallas_call(middle_kernel, out_shape=(MESSAGE, jax.ShapeDtypeStruct((M...]
  transfers between devices with their start and end apart: 1 -> 0, of which waited for: 1 -> 0; matrix products, arithmetic and copies ran while one was open for 0% -> 0% of each run, Pallas kernels for 6% -> 0%
where the time goes in v5:
time: 30.9 us; the launch traced here: 30.7 us
  blocking collectives  23.8 us (77%)
  Pallas kernels  6.22 us (20%)
  between operations  0.66 us (2%)
    all_to_all x2, blocking collectives, exchange(): lax.all_to_all(rows, 'ctx', 0, 0, axis_index_groups=groups, tiled=True)  23.8 us
    pallas_call x1, Pallas kernels, shards(): pl.pallas_call(summary_kernel, out_shape=(packed, MESSAGE, jax.ShapeDtype...  2.47 us
    pallas_call x1, Pallas kernels, shards(): pl.pallas_call(middle_kernel, out_shape=(MESSAGE, jax.ShapeDtypeStruct((M...  2.06 us
    pallas_call x1, Pallas kernels, shards(): pl.pallas_call(final_kernel, out_shape=(wide, wide, wide, jax.ShapeDtypeS...  1.69 us

profile of v5, /device:TPU:6, one launch (start us, length us, event | category | flops | bytes accessed | tf_op | source)
XLA Modules:
  0.0 30.7 jit_solution(2945980551907051071)
XLA Ops:
  0.6 2.5 %summary.1 = (f32[1352,128]{1,0:T(8,128)S(1)}, f32[200,128]{1,0:T(8,128)S(1)}, f32[2,16,128]{2,1,0:T(8,128)S(1)}) custom-call(bf16[64,1024]{1,0:T(8,128)(2,1)} %q_any.1, bf16[64,1024]{1,0:T(8,128)(2,1)} %refs_9_.1, bf16[64,1024]{1,0:T(8,128)(2,1)} %refs_10_.1, bf16[64,1024]{1,0:T(8,128)(2,1)} %refs_11_.1, f32[16,64]{1,0:T(8,128)} %bitcast.17, ...), custom_call_target="tpu_custom_call" | custom-call | tf_op jit(solution)/shard_map/summary/pallas_call | solution.py:428
  3.1 9.0 %all_to_all.10 = f32[200,1,128]{2,1,0:T(1,128)S(1)} all-to-all(f32[200,1,128]{2,1,0:T(1,128)S(1)} %bitcast.16), channel_id=1, replica_groups={{40,48,56,0,8,16,24,32},{104,112,120,64,72,80,88,96},{168,176,184,128,1..., dimensions={0} | all-to-all | bytes 204800 | tf_op jit(solution)/shard_map/all_to_all | solution.py:411
  12.1 0.0 copy-start.1
  12.1 0.0 copy-start.2
  12.1 2.1 %middle.1 = (f32[200,128]{1,0:T(8,128)S(1)}, f32[16,128]{1,0:T(8,128)S(1)}, f32[64,1024]{1,0:T(8,128)S(1)}, f32[64,1024]{1,0:T(8,128)S(1)}, f32[16,64,128]{2,1,0...) custom-call(f32[200,128]{1,0:T(8,128)S(1)} %bitcast.13, ...), custom_call_target="tpu_custom_call" | custom-call | tf_op jit(solution)/shard_map/middle/pallas_call | solution.py:445
  14.2 0.0 copy-start
  14.2 14.8 %all_to_all.11 = f32[200,1,128]{2,1,0:T(1,128)S(1)} all-to-all(f32[200,1,128]{2,1,0:T(1,128)S(1)} %bitcast.15), channel_id=1, replica_groups={{320,384,448,0,64,128,192,256},{328,392,456,8,72,136,200,264},{336,400,..., dimensions={0} | all-to-all | bytes 204800 | tf_op jit(solution)/shard_map/all_to_all | solution.py:411
  29.0 0.0 copy-done.1
  29.0 0.0 copy-done.2
  29.0 0.0 copy-done
  29.0 1.7 %final.1 = (bf16[64,1024]{1,0:T(8,128)(2,1)}, bf16[64,1024]{1,0:T(8,128)(2,1)}, bf16[64,1024]{1,0:T(8,128)(2,1)}, f32[16,64]{1,0:T(8,128)}, f32[1,64]{1,0:T(1,128)}) custom-call(f32[200,128]{1,0:T(8,128)S(1)} %bitcast.14, f32[16,128]{1,0:T(8,128)S(1)} %get-tuple-element.25.refs_1_, f32[1352,128]{1,0:T(8,128)S(1)} %get-tuple-element.23.pack_ref.refs_2_, ...), custom_call_target="tpu_custom_call" | custom-call | tf_op jit(solution)/shard_map/final/pallas_call | solution.py:455
Async XLA Ops:
  12.1 16.9 %copy-start.1 = (bf16[64,1024]{1,0:T(8,128)(2,1)S(1)}, bf16[64,1024]{1,0:T(8,128)(2,1)}, u32[]{:S(2)}) copy-start(bf16[64,1024]{1,0:T(8,128)(2,1)} %refs_10_.1) | copy-start | bytes 393220
  12.1 16.9 %copy-start.2 = (bf16[64,1024]{1,0:T(8,128)(2,1)S(1)}, bf16[64,1024]{1,0:T(8,128)(2,1)}, u32[]{:S(2)}) copy-start(bf16[64,1024]{1,0:T(8,128)(2,1)} %refs_11_.1) | copy-start | bytes 393220
  14.2 14.8 %copy-start = (bf16[64,1024]{1,0:T(8,128)(2,1)S(1)}, bf16[64,1024]{1,0:T(8,128)(2,1)}, u32[]{:S(2)}) copy-start(bf16[64,1024]{1,0:T(8,128)(2,1)} %refs_9_.1) | copy-start | bytes 393220

commit v6 on v5

--- a/solution.py
+++ b/solution.py
@@ -18,7 +18,8 @@
 GROUP = 8
 EARLY = 4
 NEAR_ORDER = tuple((k + 5) % GROUP for k in range(GROUP))
-FAR_ORDER = tuple((k + 5) % GROUP for k in range(GROUP))
+FAR_ORDER = (5, 7, 6, 4, 3, 2, 1, 0)
+PARTS = 2
 TALL = 16
 UNITS = 0
 SIGNAL = UNITS + PITCH * SUB
@@ -114,17 +115,20 @@
     q_ref, k_ref, v_ref, g_ref, rate_ref, residue_ref, skip_ref,
     row_ref, decay_ref, sems,
 ):
-    pairs = (
-        (rate_any, rate_ref), (k_any, k_ref), (v_any, v_ref), (g_any, g_ref), (q_any, q_ref),
-        (residue_any, residue_ref), (skip_any, skip_ref),
-    )
-    copies = [pltpu.make_async_copy(a, b, sems.at[n]) for n, (a, b) in enumerate(pairs)]
+    small = ((rate_any, rate_ref), (residue_any, residue_ref), (skip_any, skip_ref))
+    copies = [pltpu.make_async_copy(a, b, sems.at[n]) for n, (a, b) in enumerate(small)]
+    large = ((k_any, k_ref), (v_any, v_ref), (g_any, g_ref), (q_any, q_ref))
+    for n, (a, b) in enumerate(large):
+        for part in range(PARTS):
+            rows = pl.ds(part * (HALF // PARTS), HALF // PARTS)
+            sem = sems.at[len(small) + n * PARTS + part]
+            copies.append(pltpu.make_async_copy(a.at[rows, :], b.at[rows, :], sem))
     for copy in copies:
         copy.start()
 
-    copies[0].wait()
-    copies[5].wait()
-    copies[6].wait()
+    for copy in copies[: len(small)]:
+        copy.wait()
+    copies = copies[len(small) :]
     rates = twice(rate_ref[...])
     gains = jnp.sqrt(one_minus_exp(2.0 * rates))
     skips = jnp.concatenate([skip_ref[...], skip_ref[...]], axis=1)
@@ -149,11 +153,11 @@
         decay_ref[m, 3] = jnp.where(upper, jnp.exp(-(STEPS * row_f) * r), 0.0)
         decay_ref[m, 4] = jnp.exp(-(STEPS * chunk) * r)
 
-    copies[1].wait()
-    copies[2].wait()
+    for copy in copies[: 2 * PARTS]:
+        copy.wait()
     to_steps(k_ref[...].astype(F32) * v_ref[...].astype(F32), pack_ref, UNITS)
-    copies[3].wait()
-    copies[4].wait()
+    for copy in copies[2 * PARTS :]:
+        copy.wait()
     to_steps(g_ref[...].astype(F32) * q_ref[...].astype(F32), pack_ref, SIGNAL)
 
     zero = jnp.zeros((SUB, LANES), F32)
@@ -307,9 +311,53 @@
     return lax.div(lax.axis_index("ctx"), GROUP) < EARLY
 
 
-def middle_kernel(
-    got_ref, near_ref, pack_ref, msg_ref, enter_ref, *refs
+def first_plane():
+    return lax.div(lax.axis_index("ctx"), GROUP) == 0
+
+
+def one_way(rows, unit_ref, block_ref, local_ref, enter, blocks, full_ref, half):
+    parts = [unit_ref[m, rows, :] * enter[:, m : m + 1] for m in range(MODES)]
+    for n, b in enumerate(blocks):
+        cols = slice(b * LANES, (b + 1) * LANES)
+        full_ref[half * SUB : (half + 1) * SUB, cols] = local_ref[rows, cols] + added(parts)
+        if n < len(blocks) - 1:
+            parts = [x * block_ref[m, rows, :] for m, x in enumerate(parts)]
+
+
+def halves(i):
+    for half in range(2):
+        yield half, pl.multiple_of(i * TALL + half * SUB, SUB)
+
+
+def add_forward(i, enter_cols, mixed_ref, after_ref, block_ref, g_ref, gq_ref, full_ref):
+    for half, first in halves(i):
+        rows = pl.ds(first, SUB)
+        enter = enter_cols[pl.ds(HALF + first, SUB), :]
+        one_way(rows, after_ref, block_ref, mixed_ref, enter, range(8), full_ref, half)
+    rows = pl.ds(pl.multiple_of(i * TALL, TALL), TALL)
+    for b in range(8):
+        cols = slice(b * LANES, (b + 1) * LANES)
+        mixed = full_ref[:, cols]
+        gq_ref[rows, cols] = (g_ref[rows, cols].astype(F32) * mixed).astype(jnp.bfloat16)
+
+
+def add_backward(
+    i, enter_cols, back_ref, before_ref, block_ref, k_ref, v_ref, gk_ref, gv_ref, full_ref
 ):
+    for half, first in halves(i):
+        rows = pl.ds(first, SUB)
+        enter = enter_cols[rows, :]
+        one_way(rows, before_ref, block_ref, back_ref, enter, range(7, -1, -1), full_ref, half)
+    rows = pl.ds(pl.multiple_of(i * TALL, TALL), TALL)
+    for b in range(8):
+        cols = slice(b * LANES, (b + 1) * LANES)
+        back = full_ref[:, cols]
+        gk_ref[rows, cols] = (v_ref[rows, cols].astype(F32) * back).astype(jnp.bfloat16)
+        gv_ref[rows, cols] = (k_ref[rows, cols].astype(F32) * back).astype(jnp.bfloat16)
+
+
+def middle_kernel(got_ref, near_ref, pack_ref, g_ref, msg_ref, enter_ref, *refs):
+    local, gq_ref, (steps_ref, enter_cols, full_ref) = refs[:6], refs[6], refs[7:]
     joint, sums, direct, entering = combine(
         got_ref, NEAR_ORDER, near_ref[0], near_ref[1], lax.rem(lax.axis_index("ctx"), GROUP)
     )
@@ -318,29 +366,50 @@
 
     @pl.when(starts_early())
     def _():
-        local_outputs(pack_ref, *refs)
+        local_outputs(pack_ref, *local, steps_ref)
+
+    @pl.when(first_plane())
+    def _():
+        mixed_ref, _, after_ref, _, block_ref, _ = local
+        enter_cols[...] = turned_rows(entering)
+
+        def body(i, carry):
+            add_forward(
+                i, enter_cols, mixed_ref, after_ref, block_ref, g_ref, gq_ref, full_ref
+            )
+            return carry
+
+        lax.fori_loop(0, HALF // TALL, body, 0, unroll=2)
 
 
 def final_kernel(*refs):
     got, enter, pack, *early = refs[:9]
-    rest, late, steps = refs[9:-7], refs[-7:-1], refs[-1]
-
-    @pl.when(starts_early())
+    ready, rest, late, steps = refs[9], refs[10:-7], refs[-7:-1], refs[-1]
+
+    @pl.when(first_plane())
     def _():
-        finish(got, enter, *early, *rest)
+        finish(got, enter, *early, ready, *rest)
+
+    @pl.when(jnp.logical_and(starts_early(), jnp.logical_not(first_plane())))
+    def _():
+        finish(got, enter, *early, None, *rest)
 
     @pl.when(jnp.logical_not(starts_early()))
     def _():
         local_outputs(pack, *late, steps)
-        finish(got, enter, *late, *rest)
+        finish(got, enter, *late, None, *rest)
 
 
 def finish(
     got_ref, enter_ref, mixed_ref, back_ref, after_ref, before_ref, block_ref, table_ref,
-    k_ref, v_ref, g_ref,
+    ready_ref, k_ref, v_ref, g_ref,
     gq_any, gk_any, gv_any, gr_any, gs_any,
     gq_ref, gk_ref, gv_ref, gr_ref, gs_ref, enter_cols, full_ref, sems, out_sems,
 ):
+    copies = []
+    if ready_ref is not None:
+        copies.append(pltpu.make_async_copy(ready_ref, gq_any, sems.at[2]))
+        copies[0].start()
     joint, sums, direct, outer = combine(
         got_ref, FAR_ORDER, table_ref[0], table_ref[1], lax.div(lax.axis_index("ctx"), GROUP)
     )
@@ -349,46 +418,33 @@
     gr_ref[0:SUB] = scaled[:, :HALF]
     gr_ref[SUB:MODES] = scaled[:, HALF:]
     gs_ref[...] = direct[:, :HALF] * NORM
-    copies = [
+    small = [
         pltpu.make_async_copy(gr_ref, gr_any, sems.at[0]),
         pltpu.make_async_copy(gs_ref, gs_any, sems.at[1]),
     ]
-    for copy in copies:
+    for copy in small:
         copy.start()
-
-    def one_way(rows, unit_ref, local_ref, enter, blocks, slot, half):
-        parts = [unit_ref[m, rows, :] * enter[:, m : m + 1] for m in range(MODES)]
-        for n, b in enumerate(blocks):
-            cols = slice(b * LANES, (b + 1) * LANES)
-            full_ref[slot, half * SUB : (half + 1) * SUB, cols] = local_ref[rows, cols] + added(
-                parts
-            )
-            if n < len(blocks) - 1:
-                parts = [x * block_ref[m, rows, :] for m, x in enumerate(parts)]
+    copies.extend(small)
 
     def out_copies(i):
         rows = pl.ds(pl.multiple_of(i * TALL, TALL), TALL)
-        pairs = ((gq_ref, gq_any), (gk_ref, gk_any), (gv_ref, gv_any))
+        pairs = ((gk_ref, gk_any), (gv_ref, gv_any))
+        if ready_ref is None:
+            pairs += ((gq_ref, gq_any),)
         return [
             pltpu.make_async_copy(a.at[rows, :], b.at[rows, :], out_sems.at[n, i])
             for n, (a, b) in enumerate(pairs)
         ]
 
     def body(i, carry):
-        for half in range(2):
-            first = pl.multiple_of(i * TALL + half * SUB, SUB)
-            rows = pl.ds(first, SUB)
-            enter_b = enter_cols[rows, :]
-            enter_f = enter_cols[pl.ds(HALF + first, SUB), :]
-            one_way(rows, after_ref, mixed_ref, enter_f, range(8), 0, half)
-            one_way(rows, before_ref, back_ref, enter_b, range(7, -1, -1), 1, half)
-        rows = pl.ds(pl.multiple_of(i * TALL, TALL), TALL)
-        for b in range(8):
-            cols = slice(b * LANES, (b + 1) * LANES)
-            mixed, back = full_ref[0, :, cols], full_ref[1, :, cols]
-            gq_ref[rows, cols] = (g_ref[rows, cols].astype(F32) * mixed).astype(jnp.bfloat16)
-            gk_ref[rows, cols] = (v_ref[rows, cols].astype(F32) * back).astype(jnp.bfloat16)
-            gv_ref[rows, cols] = (k_ref[rows, cols].astype(F32) * back).astype(jnp.bfloat16)
+        if ready_ref is None:
+            add_forward(
+                i, enter_cols, mixed_ref, after_ref, block_ref, g_ref, gq_ref, full_ref.at[0]
+            )
+        add_backward(
+            i, enter_cols, back_ref, before_ref, block_ref,
+            k_ref, v_ref, gk_ref, gv_ref, full_ref.at[1],
+        )
         for copy in out_copies(i):
             copy.start()
         return carry
@@ -433,7 +489,7 @@
         scratch_shapes=[held] * 4
         + [small, small, pltpu.VMEM((1, HALF), F32)]
         + [pltpu.VMEM((2 + STEPS // SUB, MODES, LANES), F32)]
-        + [pltpu.VMEM((MODES, 5, SUB, LANES), F32), pltpu.SemaphoreType.DMA((7,))],
+        + [pltpu.VMEM((MODES, 5, SUB, LANES), F32), pltpu.SemaphoreType.DMA((3 + 4 * PARTS,))],
         compiler_params=PARAMS,
         name="summary",
     )(*(pltpu.with_memory_space_constraint(x, pltpu.HBM) for x in sources))
@@ -442,15 +498,16 @@
     units = jax.ShapeDtypeStruct((MODES, HALF, LANES), F32)
     local = (natural, natural, units, units, units)
     local = local + (jax.ShapeDtypeStruct((4, MODES, LANES), F32),)
-    msg, enter, *early = pl.pallas_call(
+    msg, enter, *early, ready = pl.pallas_call(
         middle_kernel,
-        out_shape=(MESSAGE, jax.ShapeDtypeStruct((MODES, LANES), F32)) + local,
-        in_specs=[VMEM] * 3,
-        out_specs=(VMEM,) * 8,
-        scratch_shapes=[stepped],
+        out_shape=(MESSAGE, jax.ShapeDtypeStruct((MODES, LANES), F32)) + local + (wide,),
+        in_specs=[VMEM] * 4,
+        out_specs=(VMEM,) * 9,
+        scratch_shapes=[stepped, pltpu.VMEM((LANES, LANES), F32)]
+        + [pltpu.VMEM((TALL, queries.shape[1]), F32)],
         compiler_params=PARAMS,
         name="middle",
-    )(got, near_table, pack)
+    )(got, near_table, pack, grad_out)
     got = exchange(msg, far)
     grad_q, grad_k, grad_v, grad_res, grad_skip = pl.pallas_call(
         final_kernel,
@@ -461,17 +518,17 @@
             jax.ShapeDtypeStruct((MODES, HALF), F32),
             jax.ShapeDtypeStruct((1, HALF), F32),
         ),
-        in_specs=[VMEM] * 12,
+        in_specs=[VMEM] * 13,
         out_specs=(ANY,) * 5,
         scratch_shapes=[held] * 3
         + [small, pltpu.VMEM((1, HALF), F32), pltpu.VMEM((LANES, LANES), F32)]
         + [pltpu.VMEM((2, TALL, queries.shape[1]), F32)]
-        + [pltpu.SemaphoreType.DMA((2,)), pltpu.SemaphoreType.DMA((3, HALF // TALL))]
+        + [pltpu.SemaphoreType.DMA((3,)), pltpu.SemaphoreType.DMA((3, HALF // TALL))]
         + [pltpu.VMEM(x.shape, F32) for x in local]
         + [stepped],
         compiler_params=PARAMS,
         name="final",
-    )(got, enter, pack, *early, keys, values, grad_out)
+    )(got, enter, pack, *early, ready, keys, values, grad_out)
     return (grad_q, grad_k, grad_v, grad_res.T, grad_skip.reshape(HALF))
 
 

time: 30.9 us -> 30.6 us (level)
  blocking collectives: 23.8 us -> 23.2 us
    pallas_call x1, Pallas kernels: 2.06 us -> 2.64 us  [shards(): pl.pallas_call(middle_kernel, out_shape=(MESSAGE, jax.ShapeDtypeStruct((M...]
    all_to_all x2, blocking collectives: 23.8 us -> 23.2 us  [exchange(): lax.all_to_all(rows, 'ctx', 0, 0, axis_index_groups=groups, tiled=True)]
    pallas_call x1, Pallas kernels: 1.69 us -> 1.32 us  [shards(): pl.pallas_call(final_kernel, out_shape=(wide, wide, wide, jax.ShapeDtypeS...]
where the time goes in v6:
time: 30.6 us; the launch traced here: 30.3 us
  blocking collectives  23.2 us (76%)
  Pallas kernels  6.33 us (21%)
  between operations  0.67 us (2%)
    all_to_all x2, blocking collectives, exchange(): lax.all_to_all(rows, 'ctx', 0, 0, axis_index_groups=groups, tiled=True)  23.2 us
    pallas_call x1, Pallas kernels, shards(): pl.pallas_call(middle_kernel, out_shape=(MESSAGE, jax.ShapeDtypeStruct((M...  2.64 us
    pallas_call x1, Pallas kernels, shards(): pl.pallas_call(summary_kernel, out_shape=(packed, MESSAGE, jax.ShapeDtype...  2.37 us
    pallas_call x1, Pallas kernels, shards(): pl.pallas_call(final_kernel, out_shape=(wide, wide, wide, jax.ShapeDtypeS...  1.32 us

profile of v6, /device:TPU:6, one launch (start us, length us, event | category | flops | bytes accessed | tf_op | source)
XLA Modules:
  0.0 30.3 jit_solution(16627176193840933326)
XLA Ops:
  0.6 2.4 %summary.1 = (f32[1352,128]{1,0:T(8,128)S(1)}, f32[200,128]{1,0:T(8,128)S(1)}, f32[2,16,128]{2,1,0:T(8,128)S(1)}) custom-call(bf16[64,1024]{1,0:T(8,128)(2,1)} %q_any.1, bf16[64,1024]{1,0:T(8,128)(2,1)} %refs_10_.1, bf16[64,1024]{1,0:T(8,128)(2,1)} %refs_11_.1, bf16[64,1024]{1,0:T(8,128)(2,1)} %refs_12_.1, f32[16,64]{1,0:T(8,128)} %bitcast.17, ...), custom_call_target="tpu_custom_call" | custom-call | tf_op jit(solution)/shard_map/summary/pallas_call | solution.py:484
  3.0 0.0 copy-start
  3.0 9.1 %all_to_all.10 = f32[200,1,128]{2,1,0:T(1,128)S(1)} all-to-all(f32[200,1,128]{2,1,0:T(1,128)S(1)} %bitcast.16), channel_id=1, replica_groups={{40,48,56,0,8,16,24,32},{104,112,120,64,72,80,88,96},{168,176,184,128,1..., dimensions={0} | all-to-all | bytes 204800 | tf_op jit(solution)/shard_map/all_to_all | solution.py:467
  12.1 0.0 copy-done
  12.1 0.0 copy-start.2
  12.1 2.6 %middle.1 = (f32[200,128]{1,0:T(8,128)S(1)}, f32[16,128]{1,0:T(8,128)S(1)}, f32[64,1024]{1,0:T(8,128)S(1)}, f32[64,1024]{1,0:T(8,128)S(1)}, f32[16,64,128]{2,1,0...) custom-call(f32[200,128]{1,0:T(8,128)S(1)} %bitcast.13, ...), custom_call_target="tpu_custom_call" | custom-call | tf_op jit(solution)/shard_map/middle/pallas_call | solution.py:501
  14.8 0.0 copy-start.1
  14.8 14.1 %all_to_all.11 = f32[200,1,128]{2,1,0:T(1,128)S(1)} all-to-all(f32[200,1,128]{2,1,0:T(1,128)S(1)} %bitcast.15), channel_id=1, replica_groups={{320,448,384,256,192,128,64,0},{328,456,392,264,200,136,72,8},{336,464,..., dimensions={0} | all-to-all | bytes 204800 | tf_op jit(solution)/shard_map/all_to_all | solution.py:467
  28.9 0.0 copy-done.2
  28.9 0.0 copy-done.1
  28.9 1.3 %final.1 = (bf16[64,1024]{1,0:T(8,128)(2,1)}, bf16[64,1024]{1,0:T(8,128)(2,1)}, bf16[64,1024]{1,0:T(8,128)(2,1)}, f32[16,64]{1,0:T(8,128)}, f32[1,64]{1,0:T(1,128)}) custom-call(f32[200,128]{1,0:T(8,128)S(1)} %bitcast.14, f32[16,128]{1,0:T(8,128)S(1)} %get-tuple-element.26.refs_1_, f32[1352,128]{1,0:T(8,128)S(1)} %get-tuple-element.24.pack_ref.refs_2_, ...), custom_call_target="tpu_custom_call" | custom-call | tf_op jit(solution)/shard_map/final/pallas_call | solution.py:512
Async XLA Ops:
  3.0 9.1 %copy-start = (bf16[64,1024]{1,0:T(8,128)(2,1)S(1)}, bf16[64,1024]{1,0:T(8,128)(2,1)}, u32[]{:S(2)}) copy-start(bf16[64,1024]{1,0:T(8,128)(2,1)} %refs_12_.1) | copy-start | bytes 393220
  12.1 16.8 %copy-start.2 = (bf16[64,1024]{1,0:T(8,128)(2,1)S(1)}, bf16[64,1024]{1,0:T(8,128)(2,1)}, u32[]{:S(2)}) copy-start(bf16[64,1024]{1,0:T(8,128)(2,1)} %refs_11_.1) | copy-start | bytes 393220
  14.8 14.1 %copy-start.1 = (bf16[64,1024]{1,0:T(8,128)(2,1)S(1)}, bf16[64,1024]{1,0:T(8,128)(2,1)}, u32[]{:S(2)}) copy-start(bf16[64,1024]{1,0:T(8,128)(2,1)} %refs_10_.1) | copy-start | bytes 393220

commit v7 on v6

--- a/solution.py
+++ b/solution.py
@@ -191,9 +191,6 @@
         if half == 0:
             lags = found
         for n, m in enumerate(modes):
-            within = lags[SUB - 1]
-            for d in reversed(range(SUB - 1)):
-                within = factor[n] * within + lags[d]
             scan = state[n]
             for j, d in enumerate((1, 2, 4)):
                 scan = scan + decay_ref[m, j] * pltpu.roll(scan, d, 0)
@@ -205,12 +202,15 @@
             pack_ref[BACKWARD + m * SUB : BACKWARD + (m + 1) * SUB] = back[n]
             ends.append(last + row_ref[1, m : m + 1, :] * last_other)
             adjoints.append(jnp.sum(decay_ref[m, 4] * back[n], axis=0, keepdims=True))
-            cross = factor[n] * (total[n] + start * back[n])
-            totals.append(jnp.sum(within + cross, axis=0, keepdims=True))
+            totals.append(jnp.sum(total[n] + start * back[n], axis=0, keepdims=True))
     ends = jnp.concatenate(ends, axis=0)
     adjoints = jnp.concatenate(adjoints, axis=0)
-    totals = jnp.concatenate(totals, axis=0)
-    direct = jnp.sum(lags[0], axis=0, keepdims=True)
+    lags = [jnp.sum(x, axis=0, keepdims=True) for x in lags]
+    direct = lags[0]
+    within = jnp.broadcast_to(lags[SUB - 1], (MODES, LANES))
+    for d in reversed(range(SUB - 1)):
+        within = row_ref[0] * within + lags[d]
+    totals = row_ref[0] * jnp.concatenate(totals, axis=0) + within
     adjoints = adjoints + pltpu.roll(adjoints, HALF, 1)
     totals = totals + pltpu.roll(totals, HALF, 1)
     direct = direct + pltpu.roll(direct, HALF, 1)
@@ -474,7 +474,7 @@
     wide = jax.ShapeDtypeStruct(queries.shape, jnp.bfloat16)
     held = pltpu.VMEM(queries.shape, jnp.bfloat16)
 
-    stepped = pltpu.VMEM((PITCH * SUB, LANES), F32)
+    stepped = pltpu.VMEM((PITCH * SUB + STEPS, LANES), F32)
     small = pltpu.VMEM((MODES, HALF), F32)
     packed = jax.ShapeDtypeStruct((PACK, LANES), F32)
     sources = (

time: 30.6 us -> 30.6 us (level)
  no operation moved by 1% of the time
where the time goes in v7:
time: 30.6 us; the launch traced here: 30.2 us
  blocking collectives  23.2 us (76%)
  Pallas kernels  6.32 us (21%)
  between operations  0.67 us (2%)
    all_to_all x2, blocking collectives, exchange(): lax.all_to_all(rows, 'ctx', 0, 0, axis_index_groups=groups, tiled=True)  23.2 us
    pallas_call x1, Pallas kernels, shards(): pl.pallas_call(middle_kernel, out_shape=(MESSAGE, jax.ShapeDtypeStruct((M...  2.64 us
    pallas_call x1, Pallas kernels, shards(): pl.pallas_call(summary_kernel, out_shape=(packed, MESSAGE, jax.ShapeDtype...  2.36 us
    pallas_call x1, Pallas kernels, shards(): pl.pallas_call(final_kernel, out_shape=(wide, wide, wide, jax.ShapeDtypeS...  1.32 us

profile of v7, /device:TPU:6, one launch (start us, length us, event | category | flops | bytes accessed | tf_op | source)
XLA Modules:
  0.0 30.2 jit_solution(1650391435563428636)
XLA Ops:
  0.6 2.4 %summary.1 = (f32[1352,128]{1,0:T(8,128)S(1)}, f32[200,128]{1,0:T(8,128)S(1)}, f32[2,16,128]{2,1,0:T(8,128)S(1)}) custom-call(bf16[64,1024]{1,0:T(8,128)(2,1)} %q_any.1, bf16[64,1024]{1,0:T(8,128)(2,1)} %refs_10_.1, bf16[64,1024]{1,0:T(8,128)(2,1)} %refs_11_.1, bf16[64,1024]{1,0:T(8,128)(2,1)} %refs_12_.1, f32[16,64]{1,0:T(8,128)} %bitcast.17, ...), custom_call_target="tpu_custom_call" | custom-call | tf_op jit(solution)/shard_map/summary/pallas_call | solution.py:484
  3.0 0.0 copy-start
  3.0 9.1 %all_to_all.10 = f32[200,1,128]{2,1,0:T(1,128)S(1)} all-to-all(f32[200,1,128]{2,1,0:T(1,128)S(1)} %bitcast.16), channel_id=1, replica_groups={{40,48,56,0,8,16,24,32},{104,112,120,64,72,80,88,96},{168,176,184,128,1..., dimensions={0} | all-to-all | bytes 204800 | tf_op jit(solution)/shard_map/all_to_all | solution.py:467
  12.1 0.0 copy-done
  12.1 0.0 copy-start.2
  12.1 2.6 %middle.1 = (f32[200,128]{1,0:T(8,128)S(1)}, f32[16,128]{1,0:T(8,128)S(1)}, f32[64,1024]{1,0:T(8,128)S(1)}, f32[64,1024]{1,0:T(8,128)S(1)}, f32[16,64,128]{2,1,0...) custom-call(f32[200,128]{1,0:T(8,128)S(1)} %bitcast.13, ...), custom_call_target="tpu_custom_call" | custom-call | tf_op jit(solution)/shard_map/middle/pallas_call | solution.py:501
  14.8 0.0 copy-start.1
  14.8 14.1 %all_to_all.11 = f32[200,1,128]{2,1,0:T(1,128)S(1)} all-to-all(f32[200,1,128]{2,1,0:T(1,128)S(1)} %bitcast.15), channel_id=1, replica_groups={{320,448,384,256,192,128,64,0},{328,456,392,264,200,136,72,8},{336,464,..., dimensions={0} | all-to-all | bytes 204800 | tf_op jit(solution)/shard_map/all_to_all | solution.py:467
  28.9 0.0 copy-done.2
  28.9 0.0 copy-done.1
  28.9 1.3 %final.1 = (bf16[64,1024]{1,0:T(8,128)(2,1)}, bf16[64,1024]{1,0:T(8,128)(2,1)}, bf16[64,1024]{1,0:T(8,128)(2,1)}, f32[16,64]{1,0:T(8,128)}, f32[1,64]{1,0:T(1,128)}) custom-call(f32[200,128]{1,0:T(8,128)S(1)} %bitcast.14, f32[16,128]{1,0:T(8,128)S(1)} %get-tuple-element.26.refs_1_, f32[1352,128]{1,0:T(8,128)S(1)} %get-tuple-element.24.pack_ref.refs_2_, ...), custom_call_target="tpu_custom_call" | custom-call | tf_op jit(solution)/shard_map/final/pallas_call | solution.py:512
Async XLA Ops:
  3.0 9.1 %copy-start = (bf16[64,1024]{1,0:T(8,128)(2,1)S(1)}, bf16[64,1024]{1,0:T(8,128)(2,1)}, u32[]{:S(2)}) copy-start(bf16[64,1024]{1,0:T(8,128)(2,1)} %refs_12_.1) | copy-start | bytes 393220
  12.1 16.8 %copy-start.2 = (bf16[64,1024]{1,0:T(8,128)(2,1)S(1)}, bf16[64,1024]{1,0:T(8,128)(2,1)}, u32[]{:S(2)}) copy-start(bf16[64,1024]{1,0:T(8,128)(2,1)} %refs_11_.1) | copy-start | bytes 393220
  14.8 14.1 %copy-start.1 = (bf16[64,1024]{1,0:T(8,128)(2,1)S(1)}, bf16[64,1024]{1,0:T(8,128)(2,1)}, u32[]{:S(2)}) copy-start(bf16[64,1024]{1,0:T(8,128)(2,1)} %refs_10_.1) | copy-start | bytes 393220

commit v8 on v7

--- a/solution.py
+++ b/solution.py
@@ -414,18 +414,6 @@
         got_ref, FAR_ORDER, table_ref[0], table_ref[1], lax.div(lax.axis_index("ctx"), GROUP)
     )
     enter_cols[...] = turned_rows(enter_ref[...] + table_ref[2] * outer)
-    scaled = sums * packed_modes(table_ref[3])
-    gr_ref[0:SUB] = scaled[:, :HALF]
-    gr_ref[SUB:MODES] = scaled[:, HALF:]
-    gs_ref[...] = direct[:, :HALF] * NORM
-    small = [
-        pltpu.make_async_copy(gr_ref, gr_any, sems.at[0]),
-        pltpu.make_async_copy(gs_ref, gs_any, sems.at[1]),
-    ]
-    for copy in small:
-        copy.start()
-    copies.extend(small)
-
     def out_copies(i):
         rows = pl.ds(pl.multiple_of(i * TALL, TALL), TALL)
         pairs = ((gk_ref, gk_any), (gv_ref, gv_any))
@@ -449,7 +437,20 @@
             copy.start()
         return carry
 
-    lax.fori_loop(0, HALF // TALL, body, 0, unroll=4)
+    groups = HALF // TALL
+    lax.fori_loop(0, groups - 1, body, 0, unroll=groups - 1)
+    scaled = sums * packed_modes(table_ref[3])
+    gr_ref[0:SUB] = scaled[:, :HALF]
+    gr_ref[SUB:MODES] = scaled[:, HALF:]
+    gs_ref[...] = direct[:, :HALF] * NORM
+    small = [
+        pltpu.make_async_copy(gr_ref, gr_any, sems.at[0]),
+        pltpu.make_async_copy(gs_ref, gs_any, sems.at[1]),
+    ]
+    for copy in small:
+        copy.start()
+    copies.extend(small)
+    lax.fori_loop(groups - 1, groups, body, 0, unroll=True)
     for i in range(HALF // TALL):
         copies.extend(out_copies(i))
     for copy in copies:

time: 30.6 us -> 30.6 us (level)
  no operation moved by 1% of the time
where the time goes in v8:
time: 30.6 us; the launch traced here: 30.3 us
  blocking collectives  23.2 us (76%)
  Pallas kernels  6.33 us (21%)
  between operations  0.67 us (2%)
    all_to_all x2, blocking collectives, exchange(): lax.all_to_all(rows, 'ctx', 0, 0, axis_index_groups=groups, tiled=True)  23.2 us
    pallas_call x1, Pallas kernels, shards(): pl.pallas_call(middle_kernel, out_shape=(MESSAGE, jax.ShapeDtypeStruct((M...  2.64 us
    pallas_call x1, Pallas kernels, shards(): pl.pallas_call(summary_kernel, out_shape=(packed, MESSAGE, jax.ShapeDtype...  2.36 us
    pallas_call x1, Pallas kernels, shards(): pl.pallas_call(final_kernel, out_shape=(wide, wide, wide, jax.ShapeDtypeS...  1.33 us

profile of v8, /device:TPU:6, one launch (start us, length us, event | category | flops | bytes accessed | tf_op | source)
XLA Modules:
  0.0 30.3 jit_solution(5561105914020922358)
XLA Ops:
  0.6 2.4 %summary.1 = (f32[1352,128]{1,0:T(8,128)S(1)}, f32[200,128]{1,0:T(8,128)S(1)}, f32[2,16,128]{2,1,0:T(8,128)S(1)}) custom-call(bf16[64,1024]{1,0:T(8,128)(2,1)} %q_any.1, bf16[64,1024]{1,0:T(8,128)(2,1)} %refs_10_.1, bf16[64,1024]{1,0:T(8,128)(2,1)} %refs_11_.1, bf16[64,1024]{1,0:T(8,128)(2,1)} %refs_12_.1, f32[16,64]{1,0:T(8,128)} %bitcast.17, ...), custom_call_target="tpu_custom_call" | custom-call | tf_op jit(solution)/shard_map/summary/pallas_call | solution.py:485
  3.0 0.0 copy-start
  3.0 9.1 %all_to_all.10 = f32[200,1,128]{2,1,0:T(1,128)S(1)} all-to-all(f32[200,1,128]{2,1,0:T(1,128)S(1)} %bitcast.16), channel_id=1, replica_groups={{40,48,56,0,8,16,24,32},{104,112,120,64,72,80,88,96},{168,176,184,128,1..., dimensions={0} | all-to-all | bytes 204800 | tf_op jit(solution)/shard_map/all_to_all | solution.py:468
  12.1 0.0 copy-done
  12.1 0.0 copy-start.2
  12.1 2.6 %middle.1 = (f32[200,128]{1,0:T(8,128)S(1)}, f32[16,128]{1,0:T(8,128)S(1)}, f32[64,1024]{1,0:T(8,128)S(1)}, f32[64,1024]{1,0:T(8,128)S(1)}, f32[16,64,128]{2,1,0...) custom-call(f32[200,128]{1,0:T(8,128)S(1)} %bitcast.13, ...), custom_call_target="tpu_custom_call" | custom-call | tf_op jit(solution)/shard_map/middle/pallas_call | solution.py:502
  14.8 0.0 copy-start.1
  14.8 14.1 %all_to_all.11 = f32[200,1,128]{2,1,0:T(1,128)S(1)} all-to-all(f32[200,1,128]{2,1,0:T(1,128)S(1)} %bitcast.15), channel_id=1, replica_groups={{320,448,384,256,192,128,64,0},{328,456,392,264,200,136,72,8},{336,464,..., dimensions={0} | all-to-all | bytes 204800 | tf_op jit(solution)/shard_map/all_to_all | solution.py:468
  28.9 0.0 copy-done.2
  28.9 0.0 copy-done.1
  28.9 1.3 %final.1 = (bf16[64,1024]{1,0:T(8,128)(2,1)}, bf16[64,1024]{1,0:T(8,128)(2,1)}, bf16[64,1024]{1,0:T(8,128)(2,1)}, f32[16,64]{1,0:T(8,128)}, f32[1,64]{1,0:T(1,128)}) custom-call(f32[200,128]{1,0:T(8,128)S(1)} %bitcast.14, f32[16,128]{1,0:T(8,128)S(1)} %get-tuple-element.26.refs_1_, f32[1352,128]{1,0:T(8,128)S(1)} %get-tuple-element.24.pack_ref.refs_2_, ...), custom_call_target="tpu_custom_call" | custom-call | tf_op jit(solution)/shard_map/final/pallas_call | solution.py:513
Async XLA Ops:
  3.0 9.1 %copy-start = (bf16[64,1024]{1,0:T(8,128)(2,1)S(1)}, bf16[64,1024]{1,0:T(8,128)(2,1)}, u32[]{:S(2)}) copy-start(bf16[64,1024]{1,0:T(8,128)(2,1)} %refs_12_.1) | copy-start | bytes 393220
  12.1 16.8 %copy-start.2 = (bf16[64,1024]{1,0:T(8,128)(2,1)S(1)}, bf16[64,1024]{1,0:T(8,128)(2,1)}, u32[]{:S(2)}) copy-start(bf16[64,1024]{1,0:T(8,128)(2,1)} %refs_11_.1) | copy-start | bytes 393220
  14.8 14.1 %copy-start.1 = (bf16[64,1024]{1,0:T(8,128)(2,1)S(1)}, bf16[64,1024]{1,0:T(8,128)(2,1)}, u32[]{:S(2)}) copy-start(bf16[64,1024]{1,0:T(8,128)(2,1)} %refs_10_.1) | copy-start | bytes 393220
